TPU v7x, 32 devices: a whole 2x2x4 slice. The times are simulated.
32 devices in a mesh: groups: 2 (over y), dp: 16 (over z, x, core).
Axes of the slice: x: 2, y: 2, z: 4, core: 2. Of those that a mesh axis runs over, the one named last changes fastest.
Arguments:
- tokens: bfloat16 [8192, 8192], P(('groups', 'dp')), parts along dimension 0, may hold values from -6 to 6
- base_weight: bfloat16 [8192, 256], replicated, may hold values from -0.0625 to 0.0625
- panels: bfloat16 [64, 540672], P('groups', 'dp'), parts along dimension 0
- upstream: bfloat16 [8192, 256], P(('groups', 'dp')), parts along dimension 0, may hold values from -0.59765625 to 0.59765625
- seq_slot: int32 [128], P('groups'), parts along dimension 0, may hold values from 0 to 3, as said below
- device_jobs: int32 [32, 4], P('groups'), parts along dimension 0, may hold values from -1 to 31, as said below
Outputs:
- projected: bfloat16 [8192, 256], P(('groups', 'dp')), parts along dimension 0
- grads: bfloat16 [64, 540672], P('groups', 'dp'), parts along dimension 0
There are 2 independent parts, one for each index of `groups`. A program takes and returns all parts, laid end to end along the dimension named above; an argument that names none is the same for every part. Nothing has to cross between parts.
Inputs may be any that keep to these rules, and one draw needn't show every extreme that they name: `device_jobs`: row e lists the distinct jobs of device e's slots, live entries first and -1 in the unused slots after them; every row has one live slot or more, and at least one row uses all 4. `seq_slot`: each sequence names a live slot of its device's row in device_jobs, and every live slot is named by at least one sequence of that device.
All inputs are finite; a program needn't handle non-finite values.
Results may differ from a plain program's by a relative error of at most 0.0049.
Values may be sent and summed in bfloat16 or wider, within the bound.
A program may use at most 128 MiB of HBM per device.

v0:
```python
import jax
import jax.numpy as jnp
from jax import lax
from jax.sharding import PartitionSpec as P

RANK = 64


adapter_scale = 0.5


def slot_panels(panels, device_jobs, rank_size):
    count = lax.axis_size("dp")
    slot_count = device_jobs.shape[1]
    chosen = jnp.take(panels, jnp.maximum(device_jobs, 0).reshape(-1), axis=0)
    outgoing = chosen.reshape(count, slot_count, panels.shape[1])
    arrived = lax.all_to_all(outgoing, "dp", split_axis=0, concat_axis=2, tiled=True)
    return arrived.reshape(slot_count, -1, rank_size)


def local(tokens, base_weight, panels, upstream, seq_slot, device_jobs):
    count = lax.axis_size("dp")
    device = lax.axis_index("dp")
    width = tokens.shape[1]
    head_columns = base_weight.shape[1]
    rank_size = RANK
    seq_count = seq_slot.shape[0] // count
    seq_len = tokens.shape[0] // seq_count
    row_count = panels.shape[1] // rank_size
    job_total = panels.shape[0]
    my_slots = lax.dynamic_slice_in_dim(seq_slot, device * seq_count, seq_count)
    stacked = slot_panels(panels, device_jobs, rank_size)
    frozen_output = jnp.dot(tokens, base_weight, preferred_element_type=jnp.float32)
    seq_panels = jnp.take(stacked, my_slots, axis=0)
    adapter_down_rows = seq_panels[:, :width]
    bt_rows = seq_panels[:, width:]
    sequence_token_rows = tokens.reshape(seq_count, seq_len, width)
    seq_grads = upstream.reshape(seq_count, seq_len, head_columns)
    lowrank = jnp.einsum(
        "ovc,ocm->ovm", sequence_token_rows, adapter_down_rows, preferred_element_type=jnp.float32
    ).astype(jnp.bfloat16)
    adapted_output = jnp.einsum(
        "slr,shr->slh", lowrank, bt_rows, preferred_element_type=jnp.float32
    )
    projected = (frozen_output + adapter_scale * adapted_output.reshape(-1, head_columns)).astype(
        jnp.bfloat16
    )
    back_rank = jnp.einsum(
        "slh,shr->slr", seq_grads, bt_rows, preferred_element_type=jnp.float32
    ).astype(jnp.bfloat16)
    left = jnp.concatenate([tokens, upstream], axis=1)
    left_cols = lax.all_to_all(left, "dp", split_axis=1, concat_axis=0, tiled=True)
    right = jnp.concatenate([back_rank, lowrank], axis=2).reshape(-1, 2 * rank_size)
    right_all = lax.all_gather(right, "dp", axis=0, tiled=True)
    source = jnp.arange(count * seq_count) // seq_count
    owners = device_jobs[source, seq_slot]
    owners = jnp.where(owners < 0, job_total, owners)
    group = 16
    turns = count // group
    block_seqs = group * seq_count
    left_blocks = left_cols.reshape(turns, block_seqs, seq_len, row_count)
    right_blocks = right_all.reshape(turns, block_seqs, seq_len, 2 * rank_size)
    owner_blocks = owners.reshape(turns, block_seqs)
    first_row = device * row_count
    last_row = first_row + row_count - 1
    straddles = jnp.logical_and(first_row < width, last_row >= width)
    all_up = first_row >= width
    row_index = first_row + jnp.arange(row_count)
    down_rows = (row_index < width)[None, :, None]
    job_index = jnp.arange(job_total)

    def one_half(left_seq, right_seq):
        factor = jnp.where(all_up, right_seq[:, :, rank_size:], right_seq[:, :, :rank_size])
        return jnp.einsum("nlp,nlr->npr", left_seq, factor, preferred_element_type=jnp.float32)

    def two_halves(left_seq, right_seq):
        down_term = jnp.einsum(
            "nlp,nlr->npr",
            left_seq,
            right_seq[:, :, :rank_size],
            preferred_element_type=jnp.float32,
        )
        up_term = jnp.einsum(
            "nlp,nlr->npr",
            left_seq,
            right_seq[:, :, rank_size:],
            preferred_element_type=jnp.float32,
        )
        return jnp.where(down_rows, down_term, up_term)

    def accumulate(total_sums, item):
        left_seq, right_seq, owner_now = item
        term = lax.cond(straddles, two_halves, one_half, left_seq, right_seq)
        selector = (owner_now[:, None] == job_index[None, :]).astype(jnp.float32)
        added = jnp.dot(
            selector.T,
            term.reshape(block_seqs, -1),
            preferred_element_type=jnp.float32,
            precision=lax.Precision.HIGHEST,
        )
        return (total_sums + added, None)

    start = jnp.zeros((job_total, row_count * rank_size), jnp.float32)
    summed_output, unused = lax.scan(accumulate, start, (left_blocks, right_blocks, owner_blocks))
    grads = (adapter_scale * summed_output).astype(jnp.bfloat16)
    return (projected, grads)


def solution(mesh):
    in_specs = (
        P(("groups", "dp"), None),
        P(),
        P("groups", "dp"),
        P(("groups", "dp"), None),
        P("groups"),
        P("groups", None),
    )
    out_specs = (P(("groups", "dp"), None), P("groups", "dp"))
    return jax.shard_map(local, mesh=mesh, in_specs=in_specs, out_specs=out_specs, check_vma=False)
```

profile of v0, /device:TPU:31, one launch (start us, length us, event | category | flops | bytes accessed | tf_op | source)
XLA Modules:
  0.0 303.7 jit_solution(2819938032157695202)
XLA Ops:
  7.2 0.0 copy-start
  7.2 0.8 broadcast_maximum_fusion
  8.0 0.7 broadcast_compare_fusion
  8.7 0.1 copy.33
  8.8 0.1 reshape.133
  8.9 0.0 copy-done
  8.9 5.4 %gather_fusion = bf16[64,33792]{1,0:T(8,128)(2,1)} fusion(bf16[32,33792]{1,0:T(8,128)(2,1)S(1)} %copy-done, s32[1024]{0:T(1024)S(1)} %pad_clamp_fusion.1), kind=kCustom, calls=%fused_computation | custom fusion | bytes 8651008 | tf_op jit(solution)/shard_map/jit(_take)/gather | solution.py:15
  14.3 7.3 %gather.14 = bf16[16,4,33792]{2,1,0:T(4,128)(2,1)} reshape(bf16[64,33792]{1,0:T(8,128)(2,1)} %gather_fusion) | data formatting | bytes 8650752 | tf_op jit(solution)/shard_map/jit(_take)/gather | solution.py:15
  21.6 0.1 copy.32
  21.7 6.2 %broadcast_select_fusion.2 = bf16[16,4,33792]{2,1,0:T(4,128)(2,1)} fusion(bf16[16,4,33792]{2,1,0:T(4,128)(2,1)} %gather.14, pred[16,4]{1,0:T(8,128)(4,1)S(1)} %copy.32), kind=kLoop, calls=%fused_computation.16 | loop fusion | flops 2162688 | bytes 8650816 | tf_op jit(solution)/shard_map/jit(_take)/select_n | solution.py:15
  27.9 6.5 %all-to-all-start = ((bf16[16,4,33792]{2,1,0:T(4,128)(2,1)}), bf16[16,4,33792]{2,1,0:T(4,128)(2,1)}, u32[]{:S(2)}, u32[]{:S(2)}) async-start(bf16[16,4,33792]{2,1,0:T(4,128)(2,1)} %broadcast_select_fusion.2), calls=%async_computation | async-start | bytes 8650752 | tf_op jit(solution)/shard_map/all_to_all | solution.py:17
  34.4 0.0 copy-done.5
  34.4 0.1 copy.37
  34.5 6.4 %copy.36 = bf16[256,8192]{0,1:T(8,128)(2,1)} copy(bf16[256,8192]{1,0:T(8,128)(2,1)} %param.8) | data formatting | bytes 8388608 | tf_op args[0]
  40.9 8.9 %pad_maximum_fusion = bf16[256,8448]{0,1:T(8,128)(2,1)} fusion(bf16[256,256]{0,1:T(8,128)(2,1)S(1)} %copy.37, bf16[256,8192]{0,1:T(8,128)(2,1)} %copy.36), kind=kLoop, calls=%fused_computation.14 | loop fusion | flops 8650752 | bytes 8650752 | tf_op jit(solution)/shard_map/concatenate | solution.py:51
  49.7 79.0 %all-to-all-done = bf16[16,4,33792]{2,1,0:T(4,128)(2,1)} async-done(((bf16[16,4,33792]{2,1,0:T(4,128)(2,1)}), bf16[16,4,33792]{2,1,0:T(4,128)(2,1)}, u32[]{:S(2)}, u32[]{:S(2)}) %all-to-all-start) | async-done | bytes 4325408 | tf_op jit(solution)/shard_map/all_to_all | solution.py:17
  128.7 6.0 %all-to-all-start.1 = ((bf16[256,16,528]{0,2,1:T(8,128)(2,1)}), bf16[256,16,528]{0,2,1:T(8,128)(2,1)}, u32[]{:S(2)}, u32[]{:S(2)}) async-start(bf16[256,16,528]{0,2,1:T(8,128)(2,1)} %bitcast.39), calls=%async_computation.1 | async-start | bytes 8650752 | tf_op jit(solution)/shard_map/all_to_all | solution.py:52
  134.7 0.2 all-gather.2.cloned.1.call-start
  134.9 0.0 copy-done.6
  134.9 0.1 compare_and_fusion
  135.0 5.5 %copy.34 = bf16[1,4,16,33792]{3,2,1,0:T(8,128)(2,1)} copy(bf16[1,4,16,33792]{3,1,2,0:T(4,128)(2,1)} %bitcast.3) | data formatting | bytes 8650752 | tf_op jit(solution)/shard_map/all_to_all | solution.py:17
  140.5 10.2 %reshape.134 = bf16[4,8448,64]{2,1,0:T(8,128)(2,1)} reshape(bf16[1,4,16,33792]{3,2,1,0:T(8,128)(2,1)} %copy.34) | data formatting | bytes 8650752 | tf_op jit(solution)/shard_map/reshape | solution.py:18
  150.7 9.3 %copy.35 = bf16[4,8448,64]{1,2,0:T(8,128)(2,1)} copy(bf16[4,8448,64]{2,1,0:T(8,128)(2,1)} %reshape.134) | data formatting | bytes 8650752 | tf_op jit(solution)/shard_map/reshape | solution.py:18
  160.0 5.0 %gather_fusion.1 = bf16[4,8448,64]{1,2,0:T(8,128)(2,1)} fusion(bf16[4,8448,64]{1,2,0:T(8,128)(2,1)} %copy.35, s32[1024]{0:T(1024)S(1)} %pad_clamp_fusion), kind=kCustom, calls=%fused_computation.1 | custom fusion | bytes 8650768 | tf_op jit(solution)/shard_map/jit(_take)/gather | solution.py:34
  165.1 2.9 broadcast_select_fusion.1
  167.9 0.0 copy-start.3
  167.9 0.2 fusion.12
  168.1 0.4 copy-done.4
  168.6 1.2 fusion.9
  169.8 0.1 copy-done.3
  169.9 0.7 pad_maximum_fusion.1
  170.6 0.0 all-gather.2.cloned.1.call-update
  170.7 0.0 copy-done.2
  170.7 0.9 gather_fusion.2
  171.6 63.8 %all-to-all-done.1 = bf16[256,16,528]{0,2,1:T(8,128)(2,1)} async-done(((bf16[256,16,528]{0,2,1:T(8,128)(2,1)}), bf16[256,16,528]{0,2,1:T(8,128)(2,1)}, u32[]{:S(2)}, u32[]{:S(2)}) %all-to-all-start.1) | async-done | bytes 4325408 | tf_op jit(solution)/shard_map/all_to_all | solution.py:52
  235.4 7.6 %copy.38 = bf16[16,256,528]{2,1,0:T(8,128)(2,1)} copy(bf16[16,256,528]{1,2,0:T(8,128)(2,1)} %bitcast.14) | data formatting | bytes 8650752 | tf_op jit(solution)/shard_map/all_to_all | solution.py:52
  243.0 1.1 convolution_multiply_fusion.1
  244.0 5.4 %fusion.8 = bf16[256,256]{1,0:T(8,128)(2,1)} fusion(f32[256,256]{1,0:T(8,128)S(1)} %bitcast.45, bf16[256,8192]{1,0:T(8,128)(2,1)} %param.8, bf16[8192,256]{1,0:T(8,128)(2,1)} %param.9), kind=kOutput, calls=%fused_computation.21 | convolution fusion | flops 1073872896 | bytes 8781824 | tf_op jit(solution)/shard_map/dot_general | solution.py:33
  249.4 39.0 %conditional.1 = (f32[64,33792]{1,0:T(8,128)}) conditional(s32[]{:T(128)} %convert_element_type.26, (s32[]{:T(128)}, bf16[64,64,128]{2,1,0:T(8,128)(2,1)}, bf16[64,64,528]{2,1,0:T(8,128)(2,1)}) %tuple.34, (s32[]{:T(128)}, s32[1,528,1]{1,2,0:T(1,128)S(1)}, bf16[64,64,128]{2,1,0:T(8,128)(2,1)}, bf16[64,64,528]{2,1,0:T(8,128)(2,1)}) %tuple.35), branch_computations={%region_0.1_spmd, %region_1.2_spmd} | conditional | flops 555811840 | bytes 91885192 | solution.py:93
  249.4 2.1 copy.40
  251.5 0.0 slice-start.1
  251.6 4.1 %fusion.3 = f32[64,528,64]{1,2,0:T(8,128)S(1)} fusion(bf16[64,64,528]{2,1,0:T(8,128)(2,1)} %get-tuple-element.58, bf16[64,64,128]{1,2,0:T(8,128)(2,1)S(1)} %copy.40), kind=kOutput, calls=%fused_computation.9 | convolution fusion | flops 276824064 | bytes 14024704 | tf_op jit(solution)/shard_map/while/body/eval_jaxpr/cond/branch_1_fun/nlp,nlr->npr/dot_general | solution.py:77
  255.7 0.0 slice-done
  255.7 0.0 slice-done.1
  255.8 5.5 %broadcast_select_fusion = f32[64,528,64]{1,2,0:T(8,128)} fusion(f32[64,528,64]{1,2,0:T(8,128)S(1)} %fusion.3, pred[528]{0:T(1024)(128)(4,1)S(1)} %compare_reduce_fusion, bf16[64,64,528]{2,1,0:T(8,128)(2,1)S(1)} %bitcast.38, bf16[64,64,128]{1,2,0:T(8,128)(2,1)S(1)} %copy.40), kind=kOutput, calls=%fused_computation.7 | convolution fusion | flops 278986752 | bytes 25428992 | tf_op jit(solution)/shard_map/while/body/eval_jaxpr/cond/branch_1_fun/nlp,nlr->npr/dot_general | solution.py:83
  261.3 14.2 %copy.31 = f32[64,528,64]{2,1,0:T(8,128)} copy(f32[64,528,64]{1,2,0:T(8,128)} %broadcast_select_fusion) | data formatting | bytes 17301504 | tf_op jit(solution)/shard_map/while/body/eval_jaxpr/cond/branch_1_fun/jit(_where)/select_n | solution.py:89
  275.5 13.0 %reshape.127 = f32[64,33792]{1,0:T(8,128)} reshape(f32[64,528,64]{2,1,0:T(8,128)} %copy.31) | data formatting | bytes 17301504 | tf_op jit(solution)/shard_map/while/body/eval_jaxpr/reshape | solution.py:97
  288.4 8.4 %fusion.5 = bf16[32,33792]{1,0:T(8,128)(2,1)} fusion(f32[64,33792]{1,0:T(8,128)} %get-tuple-element.85, s32[64]{0:T(128)S(1)} %compare_select_fusion), kind=kOutput, calls=%fused_computation.13 | convolution fusion | flops 832636928 | bytes 10813696 | tf_op jit(solution)/shard_map/while/body/eval_jaxpr/dot_general | solution.py:95
  (16 shorter events, 0.1 us)
Async XLA Ops:
  7.2 1.7 copy-start
  27.9 6.5 %copy-start.5 = (bf16[256,256]{1,0:T(8,128)(2,1)S(1)}, bf16[256,256]{1,0:T(8,128)(2,1)}, u32[]{:S(2)}) copy-start(bf16[256,256]{1,0:T(8,128)(2,1)} %param.11) | copy-start | bytes 393220
  27.9 100.8 %all-to-all-start = ((bf16[16,4,33792]{2,1,0:T(4,128)(2,1)}), bf16[16,4,33792]{2,1,0:T(4,128)(2,1)}, u32[]{:S(2)}, u32[]{:S(2)}) async-start(bf16[16,4,33792]{2,1,0:T(4,128)(2,1)} %broadcast_select_fusion.2), calls=%async_computation | async-start | bytes 8650752 | tf_op jit(solution)/shard_map/all_to_all | solution.py:17
  128.7 6.2 %copy-start.6 = (s32[64]{0:T(128)S(1)}, s32[64]{0:T(128)}, u32[]{:S(2)}) copy-start(s32[64]{0:T(128)} %param.12) | copy-start | bytes 772
  128.7 106.7 %all-to-all-start.1 = ((bf16[256,16,528]{0,2,1:T(8,128)(2,1)}), bf16[256,16,528]{0,2,1:T(8,128)(2,1)}, u32[]{:S(2)}, u32[]{:S(2)}) async-start(bf16[256,16,528]{0,2,1:T(8,128)(2,1)} %bitcast.39), calls=%async_computation.1 | async-start | bytes 8650752 | tf_op jit(solution)/shard_map/all_to_all | solution.py:52
  134.7 114.7 %all-gather.2.cloned.1.call-start = ((), (), s32[]{:S(2)}) async-start(), calls=%async_computation.2 | async-start | bytes 1114112 | tf_op jit(solution)/shard_map/all_gather | solution.py:54
  165.1 3.5 %copy-start.4 = (bf16[256,8192]{1,0:T(8,128)(2,1)S(1)}, bf16[256,8192]{1,0:T(8,128)(2,1)}, u32[]{:S(2)}) copy-start(bf16[256,8192]{1,0:T(8,128)(2,1)} %param.8) | copy-start | bytes 12582916
  167.9 2.0 copy-start.3
  168.6 2.1 copy-start.2
  249.4 6.3 %slice-start = ((s8[5242880]{0:T(1024)(128)(4,1)}), s8[1048576]{0:T(1024)(128)(4,1)S(1)}, s32[]{:S(2)}) async-start(s8[5242880]{0:T(1024)(128)(4,1)} %bitcast.37), calls=%async_computation.3 | async-start | bytes 2097152 | tf_op jit(solution)/shard_map/while/body/eval_jaxpr/cond
  251.5 4.2 %slice-start.1 = ((s8[5242880]{0:T(1024)(128)(4,1)}), s8[4194304]{0:T(1024)(128)(4,1)S(1)}, s32[]{:S(2)}) async-start(s8[5242880]{0:T(1024)(128)(4,1)} %bitcast.37), calls=%async_computation.4 | async-start | bytes 8388608 | tf_op jit(solution)/shard_map/while/body/eval_jaxpr/cond
  288.4 8.4 %copy-start.1 = (bf16[32,33792]{1,0:T(8,128)(2,1)S(1)}, bf16[32,33792]{1,0:T(8,128)(2,1)}, u32[]{:S(2)}) copy-start(bf16[32,33792]{1,0:T(8,128)(2,1)} %param.10) | copy-start | bytes 6488068
Sparse Core Ops, SparseCore 0:
  170.8 60.3 all-gather.1
where the time goes:
time: 305 us; the launch traced here: 304 us
  waiting for transfers between devices  143 us (47%)
  local copies, waits for them, and re-layouts  87.8 us (29%)
  matrix products  25.9 us (8%)
  other arithmetic  20.3 us (7%)
  between operations  14.2 us (5%)
  starting transfers between devices  12.7 us (4%)
    all_to_all x1, waiting for transfers between devices, slot_panels(): lax.all_to_all(outgoing, 'dp', split_axis=0, concat_axis=2, tiled=True)  79 us
    all_to_all x1, waiting for transfers between devices, local(): lax.all_to_all(left, 'dp', split_axis=1, concat_axis=0, tiled=True)  63.8 us
    reshape x2, local copies, waits for them, and re-layouts, slot_panels(): return arrived.reshape(slot_count, -1, rank_size)  19.5 us
    select_n x1, local copies, waits for them, and re-layouts, two_halves(): return jnp.where(down_rows, down_term, up_term)  14.2 us
    reshape x1, local copies, waits for them, and re-layouts, accumulate(): term.reshape(block_seqs, -1)  13 us
    gather x2, local copies, waits for them, and re-layouts, slot_panels(): chosen = jnp.take(panels, jnp.maximum(device_jobs, 0).reshape(-1), axis=0)  12.7 us
    concatenate x1, other arithmetic, local(): left = jnp.concatenate([tokens, upstream], axis=1)  8.87 us
    dot_general x1, matrix products, accumulate(): jnp.dot(selector.T, term.reshape(block_seqs, -1), preferred_element_type=...  8.4 us
  transfers between devices with their start and end apart: 3, of which 2 were waited for; matrix products, arithmetic and copies ran while one was open for 22% of the time, Pallas kernels for 0%

commit v1 on v0

v1 whole, which is shorter than its diff:
```python
import functools

import jax
import jax.numpy as jnp
from jax import lax
from jax.experimental import pallas as pl
from jax.experimental.pallas import tpu as pltpu
from jax.sharding import PartitionSpec as P

RANK = 64
CHUNKS = 2

adapter_scale = 0.5


def flip_kernel(tokens_ref, upstream_ref, *out_refs):
    width = tokens_ref.shape[1]
    step = upstream_ref.shape[1]
    part = out_refs[0].shape[1]

    @pl.loop(0, width // step)
    def _(i):
        turned = tokens_ref[:, pl.ds(pl.multiple_of(i * step, step), step)].T
        for h, out_ref in enumerate(out_refs):
            out_ref[pl.ds(pl.multiple_of(i * step, step), step), :] = turned[:, h * part : (h + 1) * part]

    turned = upstream_ref[...].T
    for h, out_ref in enumerate(out_refs):
        out_ref[pl.ds(width, step), :] = turned[:, h * part : (h + 1) * part]


def flip(tokens, upstream):
    count, width = tokens.shape
    head = upstream.shape[1]
    part = count // CHUNKS
    shape = jax.ShapeDtypeStruct((width + head, part), tokens.dtype)
    vmem = pl.BlockSpec(memory_space=pltpu.VMEM)
    return pl.pallas_call(
        flip_kernel,
        out_shape=[shape] * CHUNKS,
        in_specs=[vmem, vmem],
        out_specs=[vmem] * CHUNKS,
        compiler_params=pltpu.CompilerParams(vmem_limit_bytes=40 * 2**20),
        name="flip",
    )(tokens, upstream)


def partial_kernel(slot_count, jobs_ref, cols_ref, slot_ref, down_ref, out_ref):
    source = pl.program_id(0)
    factor = jnp.concatenate(
        [down_ref[jobs_ref[source * slot_count + s]] for s in range(slot_count)], axis=0
    )
    product = jnp.dot(factor, cols_ref[0], preferred_element_type=jnp.float32)
    slot = slot_ref[0]
    total = jnp.zeros(out_ref.shape[1:], jnp.float32)
    for s in range(slot_count):
        total += jnp.where(slot == s, product[s * RANK : (s + 1) * RANK], 0.0)
    out_ref[0] = total.astype(out_ref.dtype)


def partial_lowrank(jobs, cols, slot, down_t, slot_count):
    count, row_count, part = cols.shape
    return pl.pallas_call(
        functools.partial(partial_kernel, slot_count),
        out_shape=jax.ShapeDtypeStruct((count, RANK, part), jnp.float32),
        grid_spec=pltpu.PrefetchScalarGridSpec(
            num_scalar_prefetch=1,
            grid=(count,),
            in_specs=[
                pl.BlockSpec((1, row_count, part), lambda e, jobs: (e, 0, 0)),
                pl.BlockSpec((1, 1, part), lambda e, jobs: (e, 0, 0)),
                pl.BlockSpec(down_t.shape, lambda e, jobs: (0, 0, 0)),
            ],
            out_specs=pl.BlockSpec((1, RANK, part), lambda e, jobs: (e, 0, 0)),
        ),
        compiler_params=pltpu.CompilerParams(vmem_limit_bytes=40 * 2**20),
        cost_estimate=pl.CostEstimate(
            flops=2 * count * row_count * part * RANK * slot_count, bytes_accessed=cols.size * 2, transcendentals=0
        ),
        name="partial_lowrank",
    )(jobs, cols, slot, down_t)


def grads_kernel(slot_count, width, *refs):
    jobs_ref, first_ref = refs[:2]
    cols_refs = refs[2 : 2 + CHUNKS]
    slot_refs = refs[2 + CHUNKS : 2 + 2 * CHUNKS]
    right_refs = refs[2 + 2 * CHUNKS : 2 + 4 * CHUNKS]
    out_ref, sums = refs[2 + 4 * CHUNKS :]
    source = pl.program_id(0)
    row_count = cols_refs[0].shape[1]
    job_total = out_ref.shape[0]

    @pl.when(source == 0)
    def _():
        sums[...] = jnp.zeros_like(sums)

    def term(right_of):
        total = None
        for h in range(CHUNKS):
            slot = slot_refs[h][0]
            right = right_refs[right_of * CHUNKS + h][0]
            spread = jnp.concatenate(
                [jnp.where(slot == s, right, jnp.zeros_like(right)) for s in range(slot_count)], axis=0
            )
            product = lax.dot_general(
                cols_refs[h][0], spread, (((1,), (1,)), ((), ())), preferred_element_type=jnp.float32
            )
            total = product if total is None else total + product
        return total

    row = first_ref[0] + lax.broadcasted_iota(jnp.int32, (row_count, 1), 0)
    total = jnp.where(row < width, term(0), term(1))
    for s in range(slot_count):
        job = jobs_ref[source * slot_count + s]
        at = pl.ds(pl.multiple_of(job * row_count, 2), row_count)
        sums[at, :] += total[:, s * RANK : (s + 1) * RANK]

    @pl.when(source == pl.num_programs(0) - 1)
    def _():
        @pl.loop(0, row_count // 2)
        def _(pair):
            even = sums[pl.ds(2 * pair, job_total, stride=row_count), :]
            odd = sums[pl.ds(2 * pair + 1, job_total, stride=row_count), :]
            both = jnp.concatenate([even, odd], axis=1) * adapter_scale
            out_ref[:, pl.ds(pl.multiple_of(pair * 2 * RANK, 2 * RANK), 2 * RANK)] = both.astype(out_ref.dtype)


def all_grads(jobs, first_row, cols, slots, back, low, job_total, width, slot_count):
    count, row_count, part = cols[0].shape
    block = lambda rows: pl.BlockSpec((1, rows, part), lambda e, jobs, first: (e, 0, 0))
    return pl.pallas_call(
        functools.partial(grads_kernel, slot_count, width),
        out_shape=jax.ShapeDtypeStruct((job_total, row_count * RANK), jnp.bfloat16),
        grid_spec=pltpu.PrefetchScalarGridSpec(
            num_scalar_prefetch=2,
            grid=(count,),
            in_specs=[block(row_count)] * CHUNKS + [block(1)] * CHUNKS + [block(RANK)] * (2 * CHUNKS),
            out_specs=pl.BlockSpec((job_total, row_count * RANK), lambda e, jobs, first: (0, 0)),
            scratch_shapes=[pltpu.VMEM((job_total * row_count, RANK), jnp.float32)],
        ),
        compiler_params=pltpu.CompilerParams(vmem_limit_bytes=48 * 2**20),
        name="grads",
    )(jobs, first_row, *cols, *slots, *back, *low)


def slot_ups(panels, jobs, first_row, width, head):
    count, slot_count = jobs.shape
    job_total = panels.shape[0]
    row_count = panels.shape[1] // RANK
    kept = min(row_count, head)
    start = jnp.clip(width - first_row, 0, row_count - kept)
    rows = lax.dynamic_slice_in_dim(panels, start * RANK, kept * RANK, axis=1)
    place = first_row + start - width
    if kept < head:
        wide = jnp.pad(rows, ((0, 0), (head * RANK, head * RANK)))
        rows = lax.dynamic_slice_in_dim(
            wide, jnp.clip(head - place, 0, head + kept) * RANK, head * RANK, axis=1
        )
        live = place > -kept
    else:
        live = place >= 0
    rows = jnp.where(live, rows, jnp.zeros_like(rows))
    chosen = rows[jobs.reshape(-1)]
    mine = lax.psum_scatter(chosen, "dp", scatter_dimension=0, tiled=True)
    return mine.reshape(slot_count, head, RANK)


def local(tokens, base_weight, panels, upstream, seq_slot, device_jobs):
    count = lax.axis_size("dp")
    device = lax.axis_index("dp")
    width = tokens.shape[1]
    head = base_weight.shape[1]
    slot_count = device_jobs.shape[1]
    seq_count = seq_slot.shape[0] // count
    seq_len = tokens.shape[0] // seq_count
    job_total = panels.shape[0]
    row_count = panels.shape[1] // RANK
    part = tokens.shape[0] // CHUNKS
    first_row = device * row_count
    jobs = jnp.maximum(device_jobs, 0)
    flat_jobs = jobs.reshape(-1)

    sent = flip(tokens, upstream)
    cols = [
        lax.all_to_all(x.reshape(count, row_count, part), "dp", split_axis=0, concat_axis=0, tiled=True)
        for x in sent
    ]

    token_slot = jnp.repeat(seq_slot, seq_len).reshape(count, 1, CHUNKS, part)
    slots = [token_slot[:, :, h] for h in range(CHUNKS)]

    frozen_output = jnp.dot(tokens, base_weight, preferred_element_type=jnp.float32)
    down_t = panels.reshape(job_total, row_count, RANK).transpose(0, 2, 1)
    row_index = first_row + jnp.arange(row_count)
    down_t = jnp.where((row_index < width)[None, None, :], down_t, jnp.zeros_like(down_t))

    bt_rows = slot_ups(panels, jobs, first_row, width, head)
    my_slots = lax.dynamic_slice_in_dim(seq_slot, device * seq_count, seq_count)
    seq_bt = bt_rows[my_slots]
    seq_grads = upstream.reshape(seq_count, seq_len, head)
    back_rank = jnp.einsum(
        "slh,shr->rsl", seq_grads, seq_bt, preferred_element_type=jnp.float32
    ).astype(jnp.bfloat16)
    back_all = lax.all_gather(back_rank.reshape(RANK, CHUNKS * part), "dp", axis=0)
    back = [back_all[:, :, h * part : (h + 1) * part] for h in range(CHUNKS)]

    low, mine = [], []
    for h in range(CHUNKS):
        partial = partial_lowrank(flat_jobs, cols[h], slots[h], down_t, slot_count)
        own = lax.psum_scatter(partial, "dp", scatter_dimension=0).astype(jnp.bfloat16)
        mine.append(own)
        low.append(lax.all_gather(own, "dp", axis=0))

    grads = all_grads(
        flat_jobs, first_row.reshape(1), cols, slots, back, low, job_total, width, slot_count
    )
    lowrank = jnp.concatenate(mine, axis=1).reshape(RANK, seq_count, seq_len)
    adapted = jnp.einsum("rsl,shr->slh", lowrank, seq_bt, preferred_element_type=jnp.float32)
    projected = (frozen_output + adapter_scale * adapted.reshape(-1, head)).astype(jnp.bfloat16)
    return projected, grads


def solution(mesh):
    in_specs = (
        P(("groups", "dp"), None),
        P(),
        P("groups", "dp"),
        P(("groups", "dp"), None),
        P("groups"),
        P("groups", None),
    )
    out_specs = (P(("groups", "dp"), None), P("groups", "dp"))
    return jax.shard_map(local, mesh=mesh, in_specs=in_specs, out_specs=out_specs, check_vma=False)
```

time: 305 us -> 393 us (1.29); the launches traced: 304 us -> 386 us
  local copies, waits for them, and re-layouts: 87.8 us -> 24.6 us
  waiting for transfers between devices: 143 us -> 206 us
  blocking collectives: 0 us -> 58.9 us
  Pallas kernels: 0 us -> 58.1 us
  matrix products: 25.9 us -> 5.84 us
  other arithmetic: 20.3 us -> 5.4 us
    unnamed x1 -> x4, waiting for transfers between devices: 0.02 us -> 96 us
    all_to_all x2, waiting for transfers between devices: 143 us -> 47.6 us  [local(): lax.all_to_all(x.reshape(count, row_count, part), 'dp', split_axis=0, con...]
    reduce_scatter x0 -> x2, waiting for transfers between devices: none -> 62.8 us  [local(): lax.psum_scatter(partial, 'dp', scatter_dimension=0).astype(jnp.bfloat16)]
    all_gather x0 -> x3, blocking collectives: none -> 58.9 us  [the longest x2 39.3 us: local(): low.append(lax.all_gather(own, 'dp', axis=0))]
    pallas_call x0 -> x4, Pallas kernels: none -> 58.1 us  [the longest x1 36.5 us: all_grads(): pl.pallas_call(functools.partial(grads_kernel, slot_count, width), out_sh...]
    reshape x4 -> x6, local copies, waits for them, and re-layouts: 32.5 us -> 12.3 us  [the longest x2 11.7 us: local(): down_t = panels.reshape(job_total, row_count, RANK).transpose(0, 2, 1)]
    dot_general x6 -> x2, matrix products: 20.5 us -> 0.33 us  [the longest x1 0.17 us: local(): jnp.einsum('slh,shr->rsl', seq_grads, seq_bt, preferred_element_type=jnp....]
    gather x4 -> x2, local copies, waits for them, and re-layouts: 18.6 us -> 3.74 us  [the longest x1 3.18 us: slot_ups(): chosen = rows[jobs.reshape(-1)]]
  transfers between devices with their start and end apart: 3 -> 5, of which waited for: 2 -> 4; matrix products, arithmetic and copies ran while one was open for 22% -> 6% of each run, Pallas kernels for 0% -> 5%
where the time goes in v1:
time: 393 us; the launch traced here: 386 us
  waiting for transfers between devices  206 us (52%)
  blocking collectives  58.9 us (15%)
  Pallas kernels  58.1 us (15%)
  local copies, waits for them, and re-layouts  24.6 us (6%)
  between operations  14.6 us (4%)
  starting transfers between devices  12.5 us (3%)
  matrix products  5.84 us (1%)
  other arithmetic  5.4 us (1%)
    unnamed x4, waiting for transfers between devices  96 us
    reduce_scatter x2, waiting for transfers between devices, local(): lax.psum_scatter(partial, 'dp', scatter_dimension=0).astype(jnp.bfloat16)  62.8 us
    all_to_all x2, waiting for transfers between devices, local(): lax.all_to_all(x.reshape(count, row_count, part), 'dp', split_axis=0, con...  47.6 us
    all_gather x2, blocking collectives, local(): low.append(lax.all_gather(own, 'dp', axis=0))  39.3 us
    pallas_call x1, Pallas kernels, all_grads(): pl.pallas_call(functools.partial(grads_kernel, slot_count, width), out_sh...  36.5 us
    all_gather x1, blocking collectives, local(): lax.all_gather(back_rank.reshape(RANK, CHUNKS * part), 'dp', axis=0)  19.6 us
    pallas_call x2, Pallas kernels, partial_lowrank(): pl.pallas_call(functools.partial(partial_kernel, slot_count), out_shape=j...  18.7 us
    all_to_all x2, starting transfers between devices, local(): lax.all_to_all(x.reshape(count, row_count, part), 'dp', split_axis=0, con...  12.3 us
  transfers between devices with their start and end apart: 5, of which 4 were waited for; matrix products, arithmetic and copies ran while one was open for 6% of the time, Pallas kernels for 5%

profile of v1, /device:TPU:31, one launch (start us, length us, event | category | flops | bytes accessed | tf_op | source)
XLA Modules:
  0.0 386.4 jit_solution(9036241563849253660)
XLA Ops:
  7.2 2.2 copy-done.3
  9.4 0.9 copy-done.6
  10.3 2.9 flip.1
  13.2 1.3 copy-done.4
  14.5 1.3 copy-done.5
  15.9 6.5 %all-to-all-start.1 = ((bf16[16,528,128]{2,1,0:T(8,128)(2,1)}), bf16[16,528,128]{2,1,0:T(8,128)(2,1)S(1)}, u32[]{:S(2)}, u32[]{:S(2)}) async-start(bf16[16,528,128]{2,1,0:T(8,128)(2,1)} %bitcast.27), calls=%async_computation.2 | async-start | bytes 4325376 | tf_op jit(solution)/shard_map/all_to_all | solution.py:186
  22.4 0.1 copy.35
  22.4 0.1 reshape.82
  22.6 47.6 %all-to-all-done.1.cols_ref.refs_3_ = bf16[16,528,128]{2,1,0:T(8,128)(2,1)S(1)} async-done(((bf16[16,528,128]{2,1,0:T(8,128)(2,1)}), bf16[16,528,128]{2,1,0:T(8,128)(2,1)S(1)}, u32[]{:S(2)}, u32[]{:S(2)}) %all-to-all-start.1) | async-done | bytes 2162720 | tf_op jit(solution)/shard_map/all_to_all | solution.py:186
  70.2 5.9 %all-to-all-start = ((bf16[16,528,128]{2,1,0:T(8,128)(2,1)}), bf16[16,528,128]{2,1,0:T(8,128)(2,1)}, u32[]{:S(2)}, u32[]{:S(2)}) async-start(bf16[16,528,128]{2,1,0:T(8,128)(2,1)} %bitcast.26), calls=%async_computation | async-start | bytes 4325376 | tf_op jit(solution)/shard_map/all_to_all | solution.py:186
  76.1 0.0 all-reduce.3.cloned.1.call-start
  76.1 1.6 dynamic-slice_select_fusion
  77.7 3.2 gather_fusion
  81.0 0.0 reduce-scatter.5.cloned.1.call-start
  81.0 0.1 reshape.78.jobs_ref.refs_0_
  81.1 5.7 %reshape.80 = bf16[32,528,64]{2,1,0:T(8,128)(2,1)} reshape(bf16[32,33792]{1,0:T(8,128)(2,1)} %param.8) | data formatting | bytes 4325376 | tf_op jit(solution)/shard_map/reshape | solution.py:194
  86.8 0.1 broadcast_in_dim.26
  86.9 0.1 broadcast_in_dim.27
  87.0 0.1 broadcast_in_dim.28
  87.1 6.0 %copy.37 = bf16[32,528,64]{1,2,0:T(8,128)(2,1)} copy(bf16[32,528,64]{2,1,0:T(8,128)(2,1)} %reshape.80) | data formatting | bytes 4325376 | tf_op jit(solution)/shard_map/reshape | solution.py:194
  93.1 0.6 dynamic-slice
  94.4 0.1 compare_select_fusion
  94.5 2.2 select_bitcast_fusion.down_ref
  96.6 0.3 copy-done.1
  96.9 7.6 %partial_lowrank.3 = f32[16,64,128]{2,1,0:T(8,128)} custom-call(s32[64]{0:T(128)S(1)} %reshape.78.jobs_ref.refs_0_, bf16[16,528,128]{2,1,0:T(8,128)(2,1)S(1)} %copy-done.1, s32[16,1,128]{2,1,0:T(1,128)S(1)} %bitcast.31, bf16[32,64,528]{2,1,0:T(8,128)(2,1)S(1)} %select_bitcast_fusion.down_ref), custom_call_target="tpu_custom_call" | custom-call | flops 553648128 | bytes 2162688 | tf_op jit(solution)/shard_map/partial_lowrank/pallas_call | solution.py:63
  104.6 0.0 reduce-scatter.3.cloned.1.call-start
  104.6 95.9 %all-reduce.3.cloned.1.call-done = bf16[64,16384]{1,0:T(8,128)(2,1)} async-done(((bf16[64,16384]{1,0:T(8,128)(2,1)}), bf16[64,16384]{1,0:T(8,128)(2,1)}) %all-reduce.3.cloned.1.call-update) | async-done | bytes 2097168
  200.5 1.0 constant_dynamic-slice_fusion
  201.5 0.3 reshape.83
  201.8 0.1 copy.42
  201.9 0.6 gather_fusion.1
  202.5 11.1 %partial_lowrank.2 = f32[16,64,128]{2,1,0:T(8,128)} custom-call(s32[64]{0:T(128)S(1)} %reshape.78.jobs_ref.refs_0_, bf16[16,528,128]{2,1,0:T(8,128)(2,1)} %all-to-all-done.cols_ref.refs_2_, s32[16,1,128]{2,1,0:T(1,128)S(1)} %bitcast.29, bf16[32,64,528]{2,1,0:T(8,128)(2,1)S(1)} %select_bitcast_fusion.down_ref), custom_call_target="tpu_custom_call" | custom-call | flops 553648128 | bytes 2162688 | tf_op jit(solution)/shard_map/partial_lowrank/pallas_call | solution.py:63
  213.7 0.2 fusion.1
  213.9 0.1 copy.43
  213.9 0.1 all_gather_reshape.3
  214.0 19.6 %all_gather.11 = bf16[16,64,256]{2,1,0:T(8,128)(2,1)S(1)} all-gather(bf16[1,64,256]{2,1,0:T(8,128)(2,1)S(1)} %all_gather_reshape.3), channel_id=1, replica_groups=mesh['groups'=2,'dp'=16] {'dp'}, dimensions={0}, use_global_device_ids=true | all-gather | bytes 557056 | tf_op jit(solution)/shard_map/all_gather | solution.py:205
  233.6 0.1 fusion.7
  233.8 25.0 %reduce-scatter.5.cloned.1.call-done = f32[1,64,128]{2,1,0:T(8,128)} async-done(((f32[16,64,128]{2,1,0:T(8,128)}), f32[1,64,128]{2,1,0:T(8,128)}) %reduce-scatter.5.cloned.1.call-update) | async-done | bytes 32784 | tf_op jit(solution)/shard_map/reduce_scatter | solution.py:211
  258.7 0.8 convert_element_type.27
  259.5 0.1 copy.46
  259.6 19.7 %all_gather.13.refs_9_ = bf16[16,64,128]{2,1,0:T(8,128)(2,1)S(1)} all-gather(bf16[1,64,128]{2,1,0:T(8,128)(2,1)S(1)} %convert_element_type.27), channel_id=1, replica_groups=mesh['groups'=2,'dp'=16] {'dp'}, dimensions={0}, use_global_device_ids=true | all-gather | bytes 278528 | tf_op jit(solution)/shard_map/all_gather | solution.py:213
  279.3 37.9 %reduce-scatter.3.cloned.1.call-done = f32[1,64,128]{2,1,0:T(8,128)} async-done(((f32[16,64,128]{2,1,0:T(8,128)}), f32[1,64,128]{2,1,0:T(8,128)}) %reduce-scatter.3.cloned.1.call-update) | async-done | bytes 32784 | tf_op jit(solution)/shard_map/reduce_scatter | solution.py:211
  317.2 0.8 convert_element_type.25
  317.9 0.1 copy.45
  318.1 19.6 %all_gather.12.refs_8_ = bf16[16,64,128]{2,1,0:T(8,128)(2,1)S(1)} all-gather(bf16[1,64,128]{2,1,0:T(8,128)(2,1)S(1)} %convert_element_type.25), channel_id=1, replica_groups=mesh['groups'=2,'dp'=16] {'dp'}, dimensions={0}, use_global_device_ids=true | all-gather | bytes 278528 | tf_op jit(solution)/shard_map/all_gather | solution.py:213
  337.7 0.2 convolution_multiply_fusion
  337.8 5.5 %fusion = bf16[256,256]{1,0:T(8,128)(2,1)} fusion(f32[256,256]{1,0:T(8,128)S(1)} %bitcast.33, bf16[256,8192]{1,0:T(8,128)(2,1)} %tokens_ref.1, bf16[8192,256]{1,0:T(8,128)(2,1)} %param.7), kind=kOutput, calls=%fused_computation.5 | convolution fusion | flops 1073872896 | bytes 8781824 | tf_op jit(solution)/shard_map/dot_general | solution.py:193
  343.4 36.5 %grads.1 = bf16[32,33792]{1,0:T(8,128)(2,1)} custom-call(s32[64]{0:T(128)S(1)} %reshape.78.jobs_ref.refs_0_, s32[1]{0:T(128)} %bitcast.10.refs_1_, bf16[16,528,128]{2,1,0:T(8,128)(2,1)} %all-to-all-done.cols_ref.refs_2_, bf16[16,528,128]{2,1,0:T(8,128)(2,1)S(1)} %copy-done.2, s32[16,1,128]{2,1,0:T(1,128)S(1)} %bitcast.30, s32[16,1,128]{2,1,0:T(1,128)S(1)} %bitcast.32, ...), custom_call_target="tpu_custom_call" | custom-call | tf_op jit(solution)/shard_map/grads/pallas_call | solution.py:132
  (28 shorter events, 0.1 us)
Async XLA Ops:
  7.2 2.2 copy-start.3
  9.4 0.9 copy-start.6
  13.2 1.3 copy-start.4
  14.5 1.3 copy-start.5
  15.9 6.5 %copy-start.8 = (s32[16,4]{0,1:T(4,128)S(1)}, s32[16,4]{0,1:T(4,128)}, u32[]{:S(2)}) copy-start(s32[16,4]{0,1:T(4,128)} %param.11) | copy-start | bytes 772
  15.9 54.3 %all-to-all-start.1 = ((bf16[16,528,128]{2,1,0:T(8,128)(2,1)}), bf16[16,528,128]{2,1,0:T(8,128)(2,1)S(1)}, u32[]{:S(2)}, u32[]{:S(2)}) async-start(bf16[16,528,128]{2,1,0:T(8,128)(2,1)} %bitcast.27), calls=%async_computation.2 | async-start | bytes 4325376 | tf_op jit(solution)/shard_map/all_to_all | solution.py:186
  70.2 7.5 %copy-start = (bf16[16,528,128]{2,1,0:T(8,128)(2,1)}, bf16[16,528,128]{2,1,0:T(8,128)(2,1)S(1)}, u32[]{:S(2)}) copy-start(bf16[16,528,128]{2,1,0:T(8,128)(2,1)S(1)} %all-to-all-done.1.cols_ref.refs_3_) | copy-start | bytes 6488068
  70.2 132.3 %all-to-all-start = ((bf16[16,528,128]{2,1,0:T(8,128)(2,1)}), bf16[16,528,128]{2,1,0:T(8,128)(2,1)}, u32[]{:S(2)}, u32[]{:S(2)}) async-start(bf16[16,528,128]{2,1,0:T(8,128)(2,1)} %bitcast.26), calls=%async_computation | async-start | bytes 4325376 | tf_op jit(solution)/shard_map/all_to_all | solution.py:186
  76.1 124.4 %all-reduce.3.cloned.1.call-start = ((), (), s32[]{:S(2)}) async-start(), calls=%async_computation.6 | async-start | bytes 4194304
  81.0 177.8 %reduce-scatter.5.cloned.1.call-start = ((), (), s32[]{:S(2)}) async-start(), calls=%async_computation.5 | async-start | bytes 557056 | tf_op jit(solution)/shard_map/reduce_scatter | solution.py:211
  81.1 5.7 %copy-start.9 = (s32[64]{0:T(128)S(1)}, s32[64]{0:T(128)}, u32[]{:S(2)}) copy-start(s32[64]{0:T(128)} %param.10) | copy-start | bytes 772
  87.1 6.0 %copy-start.10 = (u32[32]{0:T(128)S(1)}, u32[32]{0:T(128)}, u32[]{:S(2)}) copy-start(u32[32]{0:T(128)} %constant.10) | copy-start | bytes 388
  94.5 2.4 copy-start.1
  104.6 212.6 %reduce-scatter.3.cloned.1.call-start = ((), (), s32[]{:S(2)}) async-start(), calls=%async_computation.4 | async-start | bytes 557056 | tf_op jit(solution)/shard_map/reduce_scatter | solution.py:211
  202.5 11.2 %copy-start.7 = (bf16[256,256]{1,0:T(8,128)(2,1)S(1)}, bf16[256,256]{1,0:T(8,128)(2,1)}, u32[]{:S(2)}) copy-start(bf16[256,256]{1,0:T(8,128)(2,1)} %upstream_ref.1) | copy-start | bytes 393220
  337.8 5.5 %copy-start.2 = (bf16[16,528,128]{2,1,0:T(8,128)(2,1)S(1)}, bf16[16,528,128]{2,1,0:T(8,128)(2,1)}, u32[]{:S(2)}) copy-start(bf16[16,528,128]{2,1,0:T(8,128)(2,1)} %copy-done) | copy-start | bytes 6488068
Sparse Core Ops, SparseCore 0:
  81.1 119.3 all-reduce.2
  204.5 54.1 reduce-scatter.4
  262.3 54.8 reduce-scatter.2

commit v2 on v0

--- a/solution.py
+++ b/solution.py
@@ -1,6 +1,10 @@
+import functools
+
 import jax
 import jax.numpy as jnp
 from jax import lax
+from jax.experimental import pallas as pl
+from jax.experimental.pallas import tpu as pltpu
 from jax.sharding import PartitionSpec as P
 
 RANK = 64
@@ -18,7 +22,7 @@
     return arrived.reshape(slot_count, -1, rank_size)
 
 
-def local(tokens, base_weight, panels, upstream, seq_slot, device_jobs):
+def plain_local(tokens, base_weight, panels, upstream, seq_slot, device_jobs):
     count = lax.axis_size("dp")
     device = lax.axis_index("dp")
     width = tokens.shape[1]
@@ -106,6 +110,368 @@
     return (projected, grads)
 
 
+def flip_kernel(tokens_ref, upstream_ref, out_ref):
+    width = tokens_ref.shape[1]
+    step = upstream_ref.shape[1]
+
+    @pl.loop(0, width // step)
+    def _(i):
+        at = pl.ds(pl.multiple_of(i * step, step), step)
+        out_ref[at, :] = tokens_ref[:, at].T
+
+    out_ref[pl.ds(width, step), :] = upstream_ref[...].T
+
+
+def flip(tokens, upstream):
+    count, width = tokens.shape
+    vmem = pl.BlockSpec(memory_space=pltpu.VMEM)
+    return pl.pallas_call(
+        flip_kernel,
+        out_shape=jax.ShapeDtypeStruct((width + upstream.shape[1], count), tokens.dtype),
+        in_specs=[vmem, vmem],
+        out_specs=vmem,
+        compiler_params=pltpu.CompilerParams(vmem_limit_bytes=40 * 2**20),
+        name="flip",
+    )(tokens, upstream)
+
+
+def pick_slots(product, slot, slot_count):
+    total = jnp.zeros((RANK, product.shape[1]), jnp.float32)
+    for s in range(slot_count):
+        total += jnp.where(slot == s, product[s * RANK : (s + 1) * RANK], 0.0)
+    return total
+
+
+def exchange_kernel(
+    owner,
+    jobs_ref,
+    sent_ref,
+    tokens_ref,
+    weight_ref,
+    up_ref,
+    down_ref,
+    slot_ref,
+    job_ref,
+    projected_ref,
+    grads_ref,
+    cols,
+    tokens,
+    weight,
+    bt,
+    up_t,
+    back,
+    part_out,
+    part_in,
+    low,
+    sums,
+    frozen,
+    cols_send,
+    cols_recv,
+    bt_send,
+    bt_recv,
+    back_send,
+    back_recv,
+    part_send,
+    part_recv,
+    low_send,
+    low_recv,
+    local_sem,
+):
+    count, row_count, tokens_here = cols.shape
+    slot_count = bt.shape[0] // RANK
+    width = tokens.shape[1]
+    job_total = grads_ref.shape[0]
+    half = job_total // 2
+    up_start = width - owner * row_count
+    up_count = row_count - up_start
+    me = lax.axis_index("dp")
+
+    def peer(k):
+        return lax.rem(me + k, count)
+
+    def cols_copy(dest):
+        return pltpu.make_async_remote_copy(
+            src_ref=sent_ref.at[pl.ds(pl.multiple_of(dest * row_count, 16), row_count)],
+            dst_ref=cols.at[me],
+            send_sem=cols_send.at[dest],
+            recv_sem=cols_recv.at[me],
+            device_id={"dp": dest},
+            device_id_type=pl.DeviceIdType.MESH,
+        )
+
+    def bt_copy(dest):
+        return pltpu.make_async_remote_copy(
+            src_ref=up_ref.at[dest],
+            dst_ref=bt,
+            send_sem=bt_send.at[dest],
+            recv_sem=bt_recv,
+            device_id={"dp": dest},
+            device_id_type=pl.DeviceIdType.MESH,
+        )
+
+    def back_copy(dest):
+        return pltpu.make_async_remote_copy(
+            src_ref=back.at[me],
+            dst_ref=back.at[me],
+            send_sem=back_send.at[dest],
+            recv_sem=back_recv.at[me],
+            device_id={"dp": dest},
+            device_id_type=pl.DeviceIdType.MESH,
+        )
+
+    def part_copy(dest):
+        return pltpu.make_async_remote_copy(
+            src_ref=part_out.at[dest],
+            dst_ref=part_in.at[me],
+            send_sem=part_send.at[dest],
+            recv_sem=part_recv.at[me],
+            device_id={"dp": dest},
+            device_id_type=pl.DeviceIdType.MESH,
+        )
+
+    def low_copy():
+        return pltpu.make_async_remote_copy(
+            src_ref=low.at[me],
+            dst_ref=low.at[me],
+            send_sem=low_send,
+            recv_sem=low_recv.at[me],
+            device_id={"dp": owner},
+            device_id_type=pl.DeviceIdType.MESH,
+        )
+
+    def arrival(buffer, sem):
+        return pltpu.make_async_copy(buffer, buffer, sem)
+
+    tokens_in = pltpu.make_async_copy(tokens_ref, tokens, local_sem.at[0])
+    weight_in = pltpu.make_async_copy(weight_ref, weight, local_sem.at[1])
+    own_in = pltpu.make_async_copy(
+        sent_ref.at[pl.ds(pl.multiple_of(me * row_count, 16), row_count)], cols.at[me], local_sem.at[2]
+    )
+    up_in = pltpu.make_async_copy(sent_ref.at[pl.ds(width, up_count)], up_t, local_sem.at[3])
+    bt_in = pltpu.make_async_copy(up_ref.at[me], bt, local_sem.at[4])
+
+    barrier = pltpu.get_barrier_semaphore()
+
+    @pl.loop(1, count)
+    def _(k):
+        pl.semaphore_signal(barrier, inc=1, device_id={"dp": peer(k)}, device_id_type=pl.DeviceIdType.MESH)
+
+    tokens_in.start()
+    weight_in.start()
+    own_in.start()
+    up_in.start()
+    pl.semaphore_wait(barrier, count - 1)
+
+    @pl.when(me == owner)
+    def _():
+        bt_in.start()
+
+        @pl.loop(1, count)
+        def _(k):
+            bt_copy(peer(k)).start()
+
+    @pl.loop(1, count)
+    def _(k):
+        cols_copy(peer(k)).start()
+
+    sums[...] = jnp.zeros_like(sums)
+    frozen[...] = jnp.zeros_like(frozen)
+    tokens_in.wait()
+    weight_in.wait()
+    depth = width // 8
+
+    @pl.loop(0, 8)
+    def _(i):
+        at = pl.ds(pl.multiple_of(i * depth, depth), depth)
+        frozen[...] += jnp.dot(tokens[:, at], weight[at, :], preferred_element_type=jnp.float32)
+
+    own_in.wait()
+    up_in.wait()
+
+    @pl.when(me == owner)
+    def _():
+        bt_in.wait()
+
+    @pl.when(me != owner)
+    def _():
+        arrival(bt, bt_recv).wait()
+
+    my_slot = slot_ref[me]
+    back[me] = pick_slots(
+        jnp.dot(bt[...], up_t[...], preferred_element_type=jnp.float32), my_slot, slot_count
+    ).astype(back.dtype)
+
+    @pl.loop(1, count)
+    def _(k):
+        back_copy(peer(k)).start()
+
+    def lowrank_part(source):
+        factor = jnp.concatenate(
+            [down_ref[jobs_ref[source * slot_count + s]] for s in range(slot_count)], axis=0
+        )
+        product = jnp.dot(factor, cols[source], preferred_element_type=jnp.float32)
+        return pick_slots(product, slot_ref[source], slot_count)
+
+    def add_grads(source, right, first, rows):
+        job = job_ref[source]
+
+        @pl.loop(0, half // 2)
+        def _(i):
+            pieces = []
+            for pair in range(2):
+                for upper in range(2):
+                    here = job == 2 * i + pair + upper * half
+                    pieces.append(jnp.where(here, right, jnp.zeros_like(right)))
+            product = lax.dot_general(
+                cols[source, pl.ds(first, rows)],
+                jnp.concatenate(pieces, axis=0),
+                (((1,), (1,)), ((), ())),
+                preferred_element_type=jnp.float32,
+            )
+            for pair in range(2):
+                at = pl.ds(pl.multiple_of((2 * i + pair) * row_count + first, 8), rows)
+                sums[at, :] += product[:, pair * 2 * RANK : (pair + 1) * 2 * RANK]
+
+    own_part = lowrank_part(me)
+    part_in[me] = own_part.astype(part_in.dtype)
+    add_grads(me, back[me], 0, row_count)
+
+    @pl.loop(1, count)
+    def _(k):
+        source = lax.rem(me - k + count, count)
+        arrival(cols.at[source], cols_recv.at[source]).wait()
+        part_out[source] = lowrank_part(source).astype(part_out.dtype)
+        part_copy(source).start()
+        arrival(back.at[source], back_recv.at[source]).wait()
+        add_grads(source, back[source], 0, row_count)
+
+    total = own_part
+    for k in range(1, count):
+        source = lax.rem(me - k + count, count)
+        arrival(part_in.at[source], part_recv.at[source]).wait()
+        total += part_in[source].astype(jnp.float32)
+    mine = total.astype(low.dtype)
+    low[me] = mine
+
+    @pl.when(me != owner)
+    def _():
+        low_copy().start()
+
+    spread = jnp.concatenate(
+        [jnp.where(my_slot == s, mine, jnp.zeros_like(mine)) for s in range(slot_count)], axis=0
+    )
+    adapted = jnp.dot(spread.T, bt[...], preferred_element_type=jnp.float32)
+    projected_ref[...] = (frozen[...] + adapter_scale * adapted).astype(projected_ref.dtype)
+
+    @pl.when(me == owner)
+    def _():
+        @pl.loop(0, half)
+        def _(i):
+            at = pl.ds(pl.multiple_of(i * row_count + up_start, 8), up_count)
+            sums[at, :] = jnp.zeros((up_count, 2 * RANK), jnp.float32)
+
+        add_grads(me, low[me], up_start, up_count)
+
+        @pl.loop(1, count)
+        def _(k):
+            source = lax.rem(me - k + count, count)
+            arrival(low.at[source], low_recv.at[source]).wait()
+            add_grads(source, low[source], up_start, up_count)
+
+    @pl.loop(0, row_count // 2)
+    def _(pair):
+        even = sums[pl.ds(2 * pair, half, stride=row_count), :]
+        odd = sums[pl.ds(2 * pair + 1, half, stride=row_count), :]
+        first = jnp.concatenate([even[:, :RANK], odd[:, :RANK]], axis=1)
+        second = jnp.concatenate([even[:, RANK:], odd[:, RANK:]], axis=1)
+        both = jnp.concatenate([first, second], axis=0) * adapter_scale
+        grads_ref[:, pl.ds(pl.multiple_of(pair * 2 * RANK, 2 * RANK), 2 * RANK)] = both.astype(
+            grads_ref.dtype
+        )
+
+    @pl.when(me == owner)
+    def _():
+        @pl.loop(1, count)
+        def _(k):
+            bt_copy(peer(k)).wait_send()
+
+    @pl.when(me != owner)
+    def _():
+        low_copy().wait_send()
+
+    @pl.loop(1, count)
+    def _(k):
+        cols_copy(peer(k)).wait_send()
+        back_copy(peer(k)).wait_send()
+        part_copy(peer(k)).wait_send()
+
+
+def local(tokens, base_weight, panels, upstream, seq_slot, device_jobs):
+    count = lax.axis_size("dp")
+    device = lax.axis_index("dp")
+    tokens_here, width = tokens.shape
+    head = base_weight.shape[1]
+    slot_count = device_jobs.shape[1]
+    seq_count = seq_slot.shape[0] // count
+    seq_len = tokens_here // seq_count
+    job_total = panels.shape[0]
+    row_count = panels.shape[1] // RANK
+    owner = count - 1
+    up_start = width - owner * row_count
+    bf16 = jnp.bfloat16
+    jobs = jnp.maximum(device_jobs, 0)
+
+    sent = flip(tokens, upstream)
+    rows_t = panels.reshape(job_total, row_count, RANK).transpose(0, 2, 1)
+    up_t = rows_t[:, :, up_start:][jobs].reshape(count, slot_count * RANK, head)
+    row_index = device * row_count + jnp.arange(row_count)
+    down_t = jnp.where((row_index < width)[None, None, :], rows_t, jnp.zeros_like(rows_t))
+    token_slot = jnp.repeat(seq_slot, seq_len).reshape(count, 1, tokens_here)
+    seq_job = jobs[jnp.arange(count * seq_count) // seq_count, seq_slot]
+    token_job = jnp.repeat(seq_job, seq_len).reshape(count, 1, tokens_here)
+
+    vmem = pl.BlockSpec(memory_space=pltpu.VMEM)
+    hbm = pl.BlockSpec(memory_space=pl.ANY)
+    dma = pltpu.SemaphoreType.DMA
+    return pl.pallas_call(
+        functools.partial(exchange_kernel, owner),
+        out_shape=(
+            jax.ShapeDtypeStruct((tokens_here, head), bf16),
+            jax.ShapeDtypeStruct((job_total, row_count * RANK), bf16),
+        ),
+        in_specs=[pl.BlockSpec(memory_space=pltpu.SMEM), hbm, hbm, hbm, hbm, vmem, vmem, vmem],
+        out_specs=(vmem, vmem),
+        scratch_shapes=[
+            pltpu.VMEM((count, row_count, tokens_here), bf16),
+            pltpu.VMEM((tokens_here, width), bf16),
+            pltpu.VMEM((width, head), bf16),
+            pltpu.VMEM((slot_count * RANK, head), bf16),
+            pltpu.VMEM((head, tokens_here), bf16),
+            pltpu.VMEM((count, RANK, tokens_here), bf16),
+            pltpu.VMEM((count, RANK, tokens_here), bf16),
+            pltpu.VMEM((count, RANK, tokens_here), bf16),
+            pltpu.VMEM((count, RANK, tokens_here), bf16),
+            pltpu.VMEM((job_total // 2 * row_count, 2 * RANK), jnp.float32),
+            pltpu.VMEM((tokens_here, head), jnp.float32),
+            dma((count,)),
+            dma((count,)),
+            dma((count,)),
+            dma,
+            dma((count,)),
+            dma((count,)),
+            dma((count,)),
+            dma((count,)),
+            dma,
+            dma((count,)),
+            dma((5,)),
+        ],
+        compiler_params=pltpu.CompilerParams(
+            collective_id=0, has_side_effects=True, vmem_limit_bytes=56 * 2**20
+        ),
+        name="exchange",
+    )(jobs.reshape(-1), sent, tokens, base_weight, up_t, down_t, token_slot, token_job)
+
+
 def solution(mesh):
     in_specs = (
         P(("groups", "dp"), None),
@@ -116,4 +482,12 @@
         P("groups", None),
     )
     out_specs = (P(("groups", "dp"), None), P("groups", "dp"))
-    return jax.shard_map(local, mesh=mesh, in_specs=in_specs, out_specs=out_specs, check_vma=False)
+
+    def chosen(tokens, base_weight, panels, upstream, seq_slot, device_jobs):
+        width, head = base_weight.shape
+        row_count = (width + head) // lax.axis_size("dp")
+        fits = row_count >= head and row_count % 16 == 0 and panels.shape[0] % 32 == 0
+        body = local if fits else plain_local
+        return body(tokens, base_weight, panels, upstream, seq_slot, device_jobs)
+
+    return jax.shard_map(chosen, mesh=mesh, in_specs=in_specs, out_specs=out_specs, check_vma=False)

time: 305 us -> 223 us (0.73)
  Pallas kernels: 0 us -> 192 us
  waiting for transfers between devices: 143 us -> 0 us
  local copies, waits for them, and re-layouts: 87.8 us -> 26.9 us
  matrix products: 25.9 us -> 0 us
  other arithmetic: 20.3 us -> 3.14 us
  between operations: 14.2 us -> 0.7 us
  starting transfers between devices: 12.7 us -> 0 us
    pallas_call x0 -> x2, Pallas kernels: none -> 192 us  [the longest x1 189 us: local(): pl.pallas_call(functools.partial(exchange_kernel, owner), out_shape=(jax....]
    all_to_all x2 -> x0, waiting for transfers between devices: 143 us -> none  [the longest x1 79 us: slot_panels(): lax.all_to_all(outgoing, 'dp', split_axis=0, concat_axis=2, tiled=True)]
    dot_general x7 -> x0, matrix products: 25.9 us -> none  [the longest x1 8.4 us: accumulate(): jnp.dot(selector.T, term.reshape(block_seqs, -1), preferred_element_type=...]
    reshape x4 -> x3, local copies, waits for them, and re-layouts: 32.5 us -> 10.9 us  [the longest x2 10.8 us: local(): rows_t = panels.reshape(job_total, row_count, RANK).transpose(0, 2, 1)]
    gather x4 -> x2, local copies, waits for them, and re-layouts: 18.6 us -> 4.1 us  [the longest x1 3.22 us: local(): up_t = rows_t[:, :, up_start:][jobs].reshape(count, slot_count * RANK, head)]
    select_n x1 -> x0, local copies, waits for them, and re-layouts: 14.2 us -> none  [two_halves(): return jnp.where(down_rows, down_term, up_term)]
    all_to_all x2 -> x0, local copies, waits for them, and re-layouts: 13.1 us -> none  [the longest x1 7.59 us: local(): lax.all_to_all(left, 'dp', split_axis=1, concat_axis=0, tiled=True)]
    all_to_all x2 -> x0, starting transfers between devices: 12.5 us -> none  [the longest x1 6.46 us: slot_panels(): lax.all_to_all(outgoing, 'dp', split_axis=0, concat_axis=2, tiled=True)]
  transfers between devices with their start and end apart: 3 -> 0, of which waited for: 2 -> 0; matrix products, arithmetic and copies ran while one was open for 22% -> 0% of each run, Pallas kernels for 0% -> 0%
where the time goes in v2:
time: 223 us; the launch traced here: 222 us
  Pallas kernels  192 us (86%)
  local copies, waits for them, and re-layouts  26.9 us (12%)
  other arithmetic  3.14 us (1%)
    pallas_call x1, Pallas kernels, local(): pl.pallas_call(functools.partial(exchange_kernel, owner), out_shape=(jax....  189 us
    reshape x2, local copies, waits for them, and re-layouts, local(): rows_t = panels.reshape(job_total, row_count, RANK).transpose(0, 2, 1)  10.8 us
    unnamed x10, local copies, waits for them, and re-layouts  8.01 us

profile of v2, /device:TPU:31, one launch (start us, length us, event | category | flops | bytes accessed | tf_op | source)
XLA Modules:
  0.0 222.4 jit_solution(12536080497891820230)
XLA Ops:
  0.6 0.7 fusion.3
  1.3 0.7 broadcast_maximum_fusion
  2.0 0.9 gather_fusion.1
  2.9 0.1 copy.9
  3.0 0.1 reshape.75.jobs_ref
  3.1 0.0 copy-start.3
  3.1 0.1 broadcast_in_dim.40
  3.2 0.7 broadcast_in_dim.36
  3.9 0.1 broadcast_in_dim.37
  4.0 0.7 broadcast_in_dim.38.slot_ref
  4.7 0.1 broadcast_in_dim.41
  4.8 0.7 broadcast_in_dim.42.job_ref
  5.5 5.7 %reshape.76 = bf16[32,528,64]{2,1,0:T(8,128)(2,1)} reshape(bf16[32,33792]{1,0:T(8,128)(2,1)} %param.8) | data formatting | bytes 4325376 | tf_op jit(solution)/shard_map/reshape | solution.py:425
  11.2 0.0 copy-done.3
  11.2 5.1 %copy.10 = bf16[32,528,64]{1,2,0:T(8,128)(2,1)S(1)} copy(bf16[32,528,64]{2,1,0:T(8,128)(2,1)} %reshape.76) | data formatting | bytes 4325376 | tf_op jit(solution)/shard_map/reshape | solution.py:425
  16.3 1.4 slice.8
  17.7 3.2 %gather_fusion = bf16[64,64,256]{2,1,0:T(8,128)(2,1)} fusion(bf16[32,64,256]{2,1,0:T(8,128)(2,1)} %slice.8, s32[1024]{0:T(1024)S(1)} %pad_clamp_fusion), kind=kCustom, calls=%fused_computation | custom fusion | bytes 4194560 | tf_op jit(solution)/shard_map/gather | solution.py:426
  20.9 0.0 copy-start.1
  20.9 0.0 copy-start.2
  20.9 1.8 broadcast_select_fusion.down_ref
  22.7 1.4 copy-done.1
  24.1 0.0 copy-done.2
  24.1 2.9 %flip.1.sent_ref = bf16[8448,256]{1,0:T(8,128)(2,1)S(1)} custom-call(bf16[256,8192]{1,0:T(8,128)(2,1)S(1)} %copy-done.1, bf16[256,256]{1,0:T(8,128)(2,1)S(1)} %copy-done.2), custom_call_target="tpu_custom_call" | custom-call | tf_op jit(solution)/shard_map/flip/pallas_call | solution.py:128
  27.0 0.0 copy-start
  27.0 2.0 copy-done
  29.0 188.7 %exchange.1 = (bf16[256,256]{1,0:T(8,128)(2,1)}, bf16[32,33792]{1,0:T(8,128)(2,1)}) custom-call(s32[64]{0:T(128)} %copy-done.3, bf16[8448,256]{1,0:T(8,128)(2,1)} %copy-done, bf16[256,8192]{1,0:T(8,128)(2,1)} %tokens_ref.3, bf16[8192,256]{1,0:T(8,128)(2,1)} %weight_ref.1, bf16[16,256,256]{2,1,0:T(8,128)(2,1)} %bitcast.10, ...), custom_call_target="tpu_custom_call" | custom-call | tf_op jit(solution)/shard_map/exchange/pallas_call | solution.py:436
  217.7 1.6 copy.13
  219.3 3.1 %copy.14 = bf16[32,33792]{1,0:T(8,128)(2,1)} copy(bf16[32,33792]{1,0:T(8,128)(2,1)} %get-tuple-element.5) | data formatting | bytes 4325376
  (2 shorter events, 0.0 us)
Async XLA Ops:
  3.1 8.1 %copy-start.3 = (s32[64]{0:T(128)}, s32[64]{0:T(128)S(1)}, u32[]{:S(2)}) copy-start(s32[64]{0:T(128)S(1)} %reshape.75.jobs_ref) | copy-start | bytes 772
  20.9 3.1 %copy-start.1 = (bf16[256,8192]{1,0:T(8,128)(2,1)S(1)}, bf16[256,8192]{1,0:T(8,128)(2,1)}, u32[]{:S(2)}) copy-start(bf16[256,8192]{1,0:T(8,128)(2,1)} %tokens_ref.3) | copy-start | bytes 12582916
  20.9 3.1 %copy-start.2 = (bf16[256,256]{1,0:T(8,128)(2,1)S(1)}, bf16[256,256]{1,0:T(8,128)(2,1)}, u32[]{:S(2)}) copy-start(bf16[256,256]{1,0:T(8,128)(2,1)} %upstream_ref.1) | copy-start | bytes 393220
  27.0 2.0 copy-start

commit v3 on v2

--- a/solution.py
+++ b/solution.py
@@ -110,31 +110,6 @@
     return (projected, grads)
 
 
-def flip_kernel(tokens_ref, upstream_ref, out_ref):
-    width = tokens_ref.shape[1]
-    step = upstream_ref.shape[1]
-
-    @pl.loop(0, width // step)
-    def _(i):
-        at = pl.ds(pl.multiple_of(i * step, step), step)
-        out_ref[at, :] = tokens_ref[:, at].T
-
-    out_ref[pl.ds(width, step), :] = upstream_ref[...].T
-
-
-def flip(tokens, upstream):
-    count, width = tokens.shape
-    vmem = pl.BlockSpec(memory_space=pltpu.VMEM)
-    return pl.pallas_call(
-        flip_kernel,
-        out_shape=jax.ShapeDtypeStruct((width + upstream.shape[1], count), tokens.dtype),
-        in_specs=[vmem, vmem],
-        out_specs=vmem,
-        compiler_params=pltpu.CompilerParams(vmem_limit_bytes=40 * 2**20),
-        name="flip",
-    )(tokens, upstream)
-
-
 def pick_slots(product, slot, slot_count):
     total = jnp.zeros((RANK, product.shape[1]), jnp.float32)
     for s in range(slot_count):
@@ -144,21 +119,24 @@
 
 def exchange_kernel(
     owner,
-    jobs_ref,
-    sent_ref,
+    seq_slot_ref,
+    device_jobs_ref,
     tokens_ref,
     weight_ref,
-    up_ref,
-    down_ref,
-    slot_ref,
-    job_ref,
+    upstream_ref,
+    panels_ref,
     projected_ref,
     grads_ref,
     cols,
     tokens,
     weight,
+    upstream,
+    panels,
+    sent_ref,
+    down_ref,
+    up_all,
+    up_ref,
     bt,
-    up_t,
     back,
     part_out,
     part_in,
@@ -186,8 +164,43 @@
     up_count = row_count - up_start
     me = lax.axis_index("dp")
 
+    group = count // 2
+    seq_count = seq_slot_ref.shape[0] // count
+    seq_len = tokens_here // seq_count
+    low_half = me < group
+    base = jnp.where(low_half, 0, group)
+    place = me - base
+
     def peer(k):
         return lax.rem(me + k, count)
+
+    def far(i):
+        return group - base + lax.rem(place + i, group)
+
+    def near(i):
+        return base + lax.rem(place + i, group)
+
+    def for_partners(act):
+        @pl.loop(0, group)
+        def _(i):
+            act(far(i))
+
+            @pl.when(i > 0)
+            def _():
+                act(near(i))
+
+    def job_at(source, slot):
+        return jnp.maximum(device_jobs_ref[source, slot], 0)
+
+    def token_rows(source):
+        seq = lax.broadcasted_iota(jnp.int32, (1, tokens_here), 1) // seq_len
+        slot = jnp.zeros((1, tokens_here), jnp.int32)
+        job = jnp.zeros((1, tokens_here), jnp.int32)
+        for q in range(seq_count):
+            slot_q = seq_slot_ref[source * seq_count + q]
+            slot = jnp.where(seq == q, slot_q, slot)
+            job = jnp.where(seq == q, job_at(source, slot_q), job)
+        return slot, job
 
     def cols_copy(dest):
         return pltpu.make_async_remote_copy(
@@ -244,11 +257,8 @@
 
     tokens_in = pltpu.make_async_copy(tokens_ref, tokens, local_sem.at[0])
     weight_in = pltpu.make_async_copy(weight_ref, weight, local_sem.at[1])
-    own_in = pltpu.make_async_copy(
-        sent_ref.at[pl.ds(pl.multiple_of(me * row_count, 16), row_count)], cols.at[me], local_sem.at[2]
-    )
-    up_in = pltpu.make_async_copy(sent_ref.at[pl.ds(width, up_count)], up_t, local_sem.at[3])
-    bt_in = pltpu.make_async_copy(up_ref.at[me], bt, local_sem.at[4])
+    upstream_in = pltpu.make_async_copy(upstream_ref, upstream, local_sem.at[2])
+    panels_in = pltpu.make_async_copy(panels_ref, panels, local_sem.at[3])
 
     barrier = pltpu.get_barrier_semaphore()
 
@@ -257,26 +267,65 @@
         pl.semaphore_signal(barrier, inc=1, device_id={"dp": peer(k)}, device_id_type=pl.DeviceIdType.MESH)
 
     tokens_in.start()
+    upstream_in.start()
+    panels_in.start()
     weight_in.start()
-    own_in.start()
-    up_in.start()
+
+    def split_pairs(first, last):
+        @pl.loop(first, last)
+        def _(pair):
+            at = pl.ds(pl.multiple_of(pair * 2 * RANK, 2 * RANK), 2 * RANK)
+            both = panels[:, at].astype(jnp.float32)
+            even = jnp.concatenate([both[:half, :RANK], both[half:, :RANK]], axis=1)
+            odd = jnp.concatenate([both[:half, RANK:], both[half:, RANK:]], axis=1)
+            sums[pl.ds(2 * pair, half, stride=row_count), :] = even
+            sums[pl.ds(2 * pair + 1, half, stride=row_count), :] = odd
+
+    tokens_in.wait()
+    upstream_in.wait()
+    step = upstream.shape[1]
+
+    @pl.loop(0, width // step)
+    def _(i):
+        at = pl.ds(pl.multiple_of(i * step, step), step)
+        sent_ref[at, :] = tokens[:, at].T
+
+    sent_ref[pl.ds(width, step), :] = upstream[...].T
+    panels_in.wait()
     pl.semaphore_wait(barrier, count - 1)
 
     @pl.when(me == owner)
     def _():
-        bt_in.start()
-
-        @pl.loop(1, count)
-        def _(k):
-            bt_copy(peer(k)).start()
-
-    @pl.loop(1, count)
-    def _(k):
-        cols_copy(peer(k)).start()
+        split_pairs(up_start // 2, row_count // 2)
+
+        @pl.loop(0, half)
+        def _(i):
+            at = pl.ds(pl.multiple_of(i * row_count + up_start, 8), up_count)
+            turned = sums[at, :].T.astype(up_all.dtype)
+            up_all[i] = turned[:RANK]
+            up_all[i + half] = turned[RANK:]
+
+        @pl.loop(0, count)
+        def _(dest):
+            for s in range(slot_count):
+                up_ref[dest, s * RANK : (s + 1) * RANK] = up_all[job_at(dest, s)]
+
+        for_partners(lambda dest: bt_copy(dest).start())
+
+    for_partners(lambda dest: cols_copy(dest).start())
+
+    split_pairs(0, row_count // 2)
+    row = me * row_count + lax.broadcasted_iota(jnp.int32, (1, row_count), 1)
+
+    @pl.loop(0, half)
+    def _(i):
+        at = pl.ds(pl.multiple_of(i * row_count, 8), row_count)
+        turned = jnp.where(row < width, sums[at, :].T, 0.0).astype(down_ref.dtype)
+        down_ref[i] = turned[:RANK]
+        down_ref[i + half] = turned[RANK:]
 
     sums[...] = jnp.zeros_like(sums)
     frozen[...] = jnp.zeros_like(frozen)
-    tokens_in.wait()
     weight_in.wait()
     depth = width // 8
 
@@ -285,65 +334,69 @@
         at = pl.ds(pl.multiple_of(i * depth, depth), depth)
         frozen[...] += jnp.dot(tokens[:, at], weight[at, :], preferred_element_type=jnp.float32)
 
-    own_in.wait()
-    up_in.wait()
+    cols[me] = sent_ref[pl.ds(pl.multiple_of(me * row_count, 16), row_count), :]
 
     @pl.when(me == owner)
     def _():
-        bt_in.wait()
+        bt[...] = up_ref[me]
 
     @pl.when(me != owner)
     def _():
         arrival(bt, bt_recv).wait()
 
-    my_slot = slot_ref[me]
+    my_slot, unused = token_rows(me)
     back[me] = pick_slots(
-        jnp.dot(bt[...], up_t[...], preferred_element_type=jnp.float32), my_slot, slot_count
+        jnp.dot(bt[...], sent_ref[pl.ds(width, step), :], preferred_element_type=jnp.float32), my_slot, slot_count
     ).astype(back.dtype)
 
-    @pl.loop(1, count)
-    def _(k):
-        back_copy(peer(k)).start()
+    for_partners(lambda dest: back_copy(dest).start())
 
     def lowrank_part(source):
         factor = jnp.concatenate(
-            [down_ref[jobs_ref[source * slot_count + s]] for s in range(slot_count)], axis=0
+            [down_ref[job_at(source, s)] for s in range(slot_count)], axis=0
         )
         product = jnp.dot(factor, cols[source], preferred_element_type=jnp.float32)
-        return pick_slots(product, slot_ref[source], slot_count)
+        return pick_slots(product, token_rows(source)[0], slot_count)
 
     def add_grads(source, right, first, rows):
-        job = job_ref[source]
-
-        @pl.loop(0, half // 2)
+        unused, job = token_rows(source)
+
+        @pl.loop(0, half // 4)
         def _(i):
-            pieces = []
-            for pair in range(2):
-                for upper in range(2):
-                    here = job == 2 * i + pair + upper * half
-                    pieces.append(jnp.where(here, right, jnp.zeros_like(right)))
-            product = lax.dot_general(
-                cols[source, pl.ds(first, rows)],
-                jnp.concatenate(pieces, axis=0),
-                (((1,), (1,)), ((), ())),
-                preferred_element_type=jnp.float32,
-            )
-            for pair in range(2):
-                at = pl.ds(pl.multiple_of((2 * i + pair) * row_count + first, 8), rows)
-                sums[at, :] += product[:, pair * 2 * RANK : (pair + 1) * 2 * RANK]
+            left = cols[source, pl.ds(first, rows)]
+            for tile in range(2):
+                pieces = []
+                for pair in range(2):
+                    for upper in range(2):
+                        here = job == 4 * i + 2 * tile + pair + upper * half
+                        pieces.append(jnp.where(here, right, jnp.zeros_like(right)))
+                product = lax.dot_general(
+                    left,
+                    jnp.concatenate(pieces, axis=0),
+                    (((1,), (1,)), ((), ())),
+                    preferred_element_type=jnp.float32,
+                )
+                for pair in range(2):
+                    at = pl.ds(pl.multiple_of((4 * i + 2 * tile + pair) * row_count + first, 8), rows)
+                    sums[at, :] += product[:, pair * 2 * RANK : (pair + 1) * 2 * RANK]
 
     own_part = lowrank_part(me)
-    part_in[me] = own_part.astype(part_in.dtype)
     add_grads(me, back[me], 0, row_count)
 
-    @pl.loop(1, count)
-    def _(k):
-        source = lax.rem(me - k + count, count)
+    def take(source):
         arrival(cols.at[source], cols_recv.at[source]).wait()
         part_out[source] = lowrank_part(source).astype(part_out.dtype)
         part_copy(source).start()
         arrival(back.at[source], back_recv.at[source]).wait()
         add_grads(source, back[source], 0, row_count)
+
+    @pl.loop(0, group)
+    def _(i):
+        take(far(group - i))
+
+        @pl.when(i > 0)
+        def _():
+            take(near(group - i))
 
     total = own_part
     for k in range(1, count):
@@ -408,29 +461,15 @@
 
 def local(tokens, base_weight, panels, upstream, seq_slot, device_jobs):
     count = lax.axis_size("dp")
-    device = lax.axis_index("dp")
     tokens_here, width = tokens.shape
     head = base_weight.shape[1]
     slot_count = device_jobs.shape[1]
-    seq_count = seq_slot.shape[0] // count
-    seq_len = tokens_here // seq_count
     job_total = panels.shape[0]
     row_count = panels.shape[1] // RANK
     owner = count - 1
-    up_start = width - owner * row_count
     bf16 = jnp.bfloat16
-    jobs = jnp.maximum(device_jobs, 0)
-
-    sent = flip(tokens, upstream)
-    rows_t = panels.reshape(job_total, row_count, RANK).transpose(0, 2, 1)
-    up_t = rows_t[:, :, up_start:][jobs].reshape(count, slot_count * RANK, head)
-    row_index = device * row_count + jnp.arange(row_count)
-    down_t = jnp.where((row_index < width)[None, None, :], rows_t, jnp.zeros_like(rows_t))
-    token_slot = jnp.repeat(seq_slot, seq_len).reshape(count, 1, tokens_here)
-    seq_job = jobs[jnp.arange(count * seq_count) // seq_count, seq_slot]
-    token_job = jnp.repeat(seq_job, seq_len).reshape(count, 1, tokens_here)
-
     vmem = pl.BlockSpec(memory_space=pltpu.VMEM)
+    smem = pl.BlockSpec(memory_space=pltpu.SMEM)
     hbm = pl.BlockSpec(memory_space=pl.ANY)
     dma = pltpu.SemaphoreType.DMA
     return pl.pallas_call(
@@ -439,14 +478,19 @@
             jax.ShapeDtypeStruct((tokens_here, head), bf16),
             jax.ShapeDtypeStruct((job_total, row_count * RANK), bf16),
         ),
-        in_specs=[pl.BlockSpec(memory_space=pltpu.SMEM), hbm, hbm, hbm, hbm, vmem, vmem, vmem],
+        in_specs=[smem, smem, hbm, hbm, hbm, hbm],
         out_specs=(vmem, vmem),
         scratch_shapes=[
             pltpu.VMEM((count, row_count, tokens_here), bf16),
             pltpu.VMEM((tokens_here, width), bf16),
             pltpu.VMEM((width, head), bf16),
+            pltpu.VMEM((tokens_here, head), bf16),
+            pltpu.VMEM((job_total, row_count * RANK), bf16),
+            pltpu.VMEM((width + head, tokens_here), bf16),
+            pltpu.VMEM((job_total, RANK, row_count), bf16),
+            pltpu.VMEM((job_total, RANK, head), bf16),
+            pltpu.VMEM((count, slot_count * RANK, head), bf16),
             pltpu.VMEM((slot_count * RANK, head), bf16),
-            pltpu.VMEM((head, tokens_here), bf16),
             pltpu.VMEM((count, RANK, tokens_here), bf16),
             pltpu.VMEM((count, RANK, tokens_here), bf16),
             pltpu.VMEM((count, RANK, tokens_here), bf16),
@@ -463,13 +507,13 @@
             dma((count,)),
             dma,
             dma((count,)),
-            dma((5,)),
+            dma((4,)),
         ],
         compiler_params=pltpu.CompilerParams(
             collective_id=0, has_side_effects=True, vmem_limit_bytes=56 * 2**20
         ),
         name="exchange",
-    )(jobs.reshape(-1), sent, tokens, base_weight, up_t, down_t, token_slot, token_job)
+    )(seq_slot, device_jobs, tokens, base_weight, upstream, panels)
 
 
 def solution(mesh):
@@ -486,7 +530,7 @@
     def chosen(tokens, base_weight, panels, upstream, seq_slot, device_jobs):
         width, head = base_weight.shape
         row_count = (width + head) // lax.axis_size("dp")
-        fits = row_count >= head and row_count % 16 == 0 and panels.shape[0] % 32 == 0
+        fits = row_count >= head and row_count % 16 == 0 and lax.axis_size("dp") % 2 == 0 and panels.shape[0] % 32 == 0
         body = local if fits else plain_local
         return body(tokens, base_weight, panels, upstream, seq_slot, device_jobs)
 

time: 223 us -> 194 us (0.87)
  local copies, waits for them, and re-layouts: 26.9 us -> 6.01 us
  Pallas kernels: 192 us -> 187 us
  other arithmetic: 3.14 us -> 0 us
    reshape x3 -> x0, local copies, waits for them, and re-layouts: 10.9 us -> none  [the longest x2 10.8 us: local(): rows_t = panels.reshape(job_total, row_count, RANK).transpose(0, 2, 1)]
    gather x2 -> x0, local copies, waits for them, and re-layouts: 4.1 us -> none  [the longest x1 3.22 us: local(): up_t = rows_t[:, :, up_start:][jobs].reshape(count, slot_count * RANK, head)]
    pallas_call x1 -> x0, Pallas kernels: 2.93 us -> none  [flip(): pl.pallas_call(flip_kernel, out_shape=jax.ShapeDtypeStruct((width + upstr...]
    broadcast_in_dim x6 -> x0, local copies, waits for them, and re-layouts: 2.39 us -> none  [the longest x3 1.54 us: local(): token_slot = jnp.repeat(seq_slot, seq_len).reshape(count, 1, tokens_here)]
    unnamed x10 -> x3, local copies, waits for them, and re-layouts: 8.01 us -> 6.01 us
where the time goes in v3:
time: 194 us; the launch traced here: 193 us
  Pallas kernels  187 us (96%)
  local copies, waits for them, and re-layouts  6.01 us (3%)
    pallas_call x1, Pallas kernels, local(): pl.pallas_call(functools.partial(exchange_kernel, owner), out_shape=(jax....  187 us
    unnamed x3, local copies, waits for them, and re-layouts  6.01 us

profile of v3, /device:TPU:31, one launch (start us, length us, event | category | flops | bytes accessed | tf_op | source)
XLA Modules:
  0.0 193.4 jit_solution(11992434925094398146)
XLA Ops:
  0.6 1.4 copy.8.device_jobs_ref
  2.0 186.8 %exchange.1 = (bf16[256,256]{1,0:T(8,128)(2,1)}, bf16[32,33792]{1,0:T(8,128)(2,1)}) custom-call(s32[64]{0:T(128)} %seq_slot_ref.1, s32[16,4]{1,0:T(8,128)} %copy.8.device_jobs_ref, bf16[256,8192]{1,0:T(8,128)(2,1)} %tokens_ref.1, bf16[8192,256]{1,0:T(8,128)(2,1)} %weight_ref.1, bf16[256,256]{1,0:T(8,128)(2,1)} %upstream_ref.1, bf16[32,33792]{1,0:T(8,128)(2,1)} %panels_ref.1), custom_call_target="tpu_custom_call" | custom-call | tf_op jit(solution)/shard_map/exchange/pallas_call | solution.py:475
  188.8 1.6 copy.11
  190.3 3.1 %copy.12 = bf16[32,33792]{1,0:T(8,128)(2,1)} copy(bf16[32,33792]{1,0:T(8,128)(2,1)} %get-tuple-element.5) | data formatting | bytes 4325376

commit v4 on v3

--- a/solution.py
+++ b/solution.py
@@ -8,6 +8,7 @@
 from jax.sharding import PartitionSpec as P
 
 RANK = 64
+PAIRS = 8
 
 
 adapter_scale = 0.5
@@ -272,20 +273,24 @@
     weight_in.start()
 
     def split_pairs(first, last):
-        @pl.loop(first, last)
-        def _(pair):
-            at = pl.ds(pl.multiple_of(pair * 2 * RANK, 2 * RANK), 2 * RANK)
-            both = panels[:, at].astype(jnp.float32)
-            even = jnp.concatenate([both[:half, :RANK], both[half:, :RANK]], axis=1)
-            odd = jnp.concatenate([both[:half, RANK:], both[half:, RANK:]], axis=1)
-            sums[pl.ds(2 * pair, half, stride=row_count), :] = even
-            sums[pl.ds(2 * pair + 1, half, stride=row_count), :] = odd
+        @pl.loop(first // PAIRS, last // PAIRS)
+        def _(block):
+            lanes = PAIRS * 2 * RANK
+            at = pl.ds(pl.multiple_of(block * lanes, lanes), lanes)
+            wide = panels[:, at].astype(jnp.float32)
+            lines = []
+            for n in range(PAIRS):
+                both = wide[:, n * 2 * RANK : (n + 1) * 2 * RANK]
+                lines.append(jnp.concatenate([both[:half, :RANK], both[half:, :RANK]], axis=1))
+                lines.append(jnp.concatenate([both[:half, RANK:], both[half:, RANK:]], axis=1))
+            for n, line in enumerate(lines):
+                sums[pl.ds(block * 2 * PAIRS + n, half, stride=row_count), :] = line
 
     tokens_in.wait()
     upstream_in.wait()
     step = upstream.shape[1]
 
-    @pl.loop(0, width // step)
+    @pl.loop(0, width // step, unroll=2)
     def _(i):
         at = pl.ds(pl.multiple_of(i * step, step), step)
         sent_ref[at, :] = tokens[:, at].T
@@ -358,17 +363,17 @@
         product = jnp.dot(factor, cols[source], preferred_element_type=jnp.float32)
         return pick_slots(product, token_rows(source)[0], slot_count)
 
-    def add_grads(source, right, first, rows):
+    def add_grads(source, right, first, rows, tiles=2):
         unused, job = token_rows(source)
 
-        @pl.loop(0, half // 4)
+        @pl.loop(0, half // (2 * tiles))
         def _(i):
             left = cols[source, pl.ds(first, rows)]
-            for tile in range(2):
+            for tile in range(tiles):
                 pieces = []
                 for pair in range(2):
                     for upper in range(2):
-                        here = job == 4 * i + 2 * tile + pair + upper * half
+                        here = job == 2 * tiles * i + 2 * tile + pair + upper * half
                         pieces.append(jnp.where(here, right, jnp.zeros_like(right)))
                 product = lax.dot_general(
                     left,
@@ -377,7 +382,7 @@
                     preferred_element_type=jnp.float32,
                 )
                 for pair in range(2):
-                    at = pl.ds(pl.multiple_of((4 * i + 2 * tile + pair) * row_count + first, 8), rows)
+                    at = pl.ds(pl.multiple_of((2 * tiles * i + 2 * tile + pair) * row_count + first, 8), rows)
                     sums[at, :] += product[:, pair * 2 * RANK : (pair + 1) * 2 * RANK]
 
     own_part = lowrank_part(me)
@@ -423,24 +428,29 @@
             at = pl.ds(pl.multiple_of(i * row_count + up_start, 8), up_count)
             sums[at, :] = jnp.zeros((up_count, 2 * RANK), jnp.float32)
 
-        add_grads(me, low[me], up_start, up_count)
+        add_grads(me, low[me], up_start, up_count, 4)
 
         @pl.loop(1, count)
         def _(k):
             source = lax.rem(me - k + count, count)
             arrival(low.at[source], low_recv.at[source]).wait()
-            add_grads(source, low[source], up_start, up_count)
-
-    @pl.loop(0, row_count // 2)
-    def _(pair):
-        even = sums[pl.ds(2 * pair, half, stride=row_count), :]
-        odd = sums[pl.ds(2 * pair + 1, half, stride=row_count), :]
-        first = jnp.concatenate([even[:, :RANK], odd[:, :RANK]], axis=1)
-        second = jnp.concatenate([even[:, RANK:], odd[:, RANK:]], axis=1)
-        both = jnp.concatenate([first, second], axis=0) * adapter_scale
-        grads_ref[:, pl.ds(pl.multiple_of(pair * 2 * RANK, 2 * RANK), 2 * RANK)] = both.astype(
-            grads_ref.dtype
-        )
+            add_grads(source, low[source], up_start, up_count, 4)
+
+    @pl.loop(0, row_count // 2 // PAIRS)
+    def _(block):
+        lines = [
+            sums[pl.ds(block * 2 * PAIRS + n, half, stride=row_count), :] * adapter_scale
+            for n in range(2 * PAIRS)
+        ]
+        firsts, seconds = [], []
+        for even, odd in zip(lines[::2], lines[1::2]):
+            firsts.append(jnp.concatenate([even[:, :RANK], odd[:, :RANK]], axis=1))
+            seconds.append(jnp.concatenate([even[:, RANK:], odd[:, RANK:]], axis=1))
+        both = jnp.concatenate(
+            [jnp.concatenate(firsts, axis=1), jnp.concatenate(seconds, axis=1)], axis=0
+        )
+        lanes = PAIRS * 2 * RANK
+        grads_ref[:, pl.ds(pl.multiple_of(block * lanes, lanes), lanes)] = both.astype(grads_ref.dtype)
 
     @pl.when(me == owner)
     def _():

time: 194 us -> 172 us (0.89)
  Pallas kernels: 187 us -> 165 us
    pallas_call x1, Pallas kernels: 187 us -> 165 us  [local(): pl.pallas_call(functools.partial(exchange_kernel, owner), out_shape=(jax....]
where the time goes in v4:
time: 172 us; the launch traced here: 171 us
  Pallas kernels  165 us (96%)
  local copies, waits for them, and re-layouts  6.01 us (3%)
    pallas_call x1, Pallas kernels, local(): pl.pallas_call(functools.partial(exchange_kernel, owner), out_shape=(jax....  165 us
    unnamed x3, local copies, waits for them, and re-layouts  6.01 us

profile of v4, /device:TPU:31, one launch (start us, length us, event | category | flops | bytes accessed | tf_op | source)
XLA Modules:
  0.0 171.5 jit_solution(6836641806331374151)
XLA Ops:
  0.6 1.4 copy.8.device_jobs_ref
  2.0 164.8 %exchange.1 = (bf16[256,256]{1,0:T(8,128)(2,1)}, bf16[32,33792]{1,0:T(8,128)(2,1)}) custom-call(s32[64]{0:T(128)} %seq_slot_ref.1, s32[16,4]{1,0:T(8,128)} %copy.8.device_jobs_ref, bf16[256,8192]{1,0:T(8,128)(2,1)} %tokens_ref.1, bf16[8192,256]{1,0:T(8,128)(2,1)} %weight_ref.1, bf16[256,256]{1,0:T(8,128)(2,1)} %upstream_ref.1, bf16[32,33792]{1,0:T(8,128)(2,1)} %panels_ref.1), custom_call_target="tpu_custom_call" | custom-call | tf_op jit(solution)/shard_map/exchange/pallas_call | solution.py:485
  166.8 1.6 copy.11
  168.4 3.1 %copy.12 = bf16[32,33792]{1,0:T(8,128)(2,1)} copy(bf16[32,33792]{1,0:T(8,128)(2,1)} %get-tuple-element.5) | data formatting | bytes 4325376

commit v5 on v4

--- a/solution.py
+++ b/solution.py
@@ -331,6 +331,23 @@
 
     sums[...] = jnp.zeros_like(sums)
     frozen[...] = jnp.zeros_like(frozen)
+    cols[me] = sent_ref[pl.ds(pl.multiple_of(me * row_count, 16), row_count), :]
+
+    @pl.when(me == owner)
+    def _():
+        bt[...] = up_ref[me]
+
+    @pl.when(me != owner)
+    def _():
+        arrival(bt, bt_recv).wait()
+
+    my_slot, unused = token_rows(me)
+    back[me] = pick_slots(
+        jnp.dot(bt[...], sent_ref[pl.ds(width, step), :], preferred_element_type=jnp.float32), my_slot, slot_count
+    ).astype(back.dtype)
+
+    for_partners(lambda dest: back_copy(dest).start())
+
     weight_in.wait()
     depth = width // 8
 
@@ -339,23 +356,6 @@
         at = pl.ds(pl.multiple_of(i * depth, depth), depth)
         frozen[...] += jnp.dot(tokens[:, at], weight[at, :], preferred_element_type=jnp.float32)
 
-    cols[me] = sent_ref[pl.ds(pl.multiple_of(me * row_count, 16), row_count), :]
-
-    @pl.when(me == owner)
-    def _():
-        bt[...] = up_ref[me]
-
-    @pl.when(me != owner)
-    def _():
-        arrival(bt, bt_recv).wait()
-
-    my_slot, unused = token_rows(me)
-    back[me] = pick_slots(
-        jnp.dot(bt[...], sent_ref[pl.ds(width, step), :], preferred_element_type=jnp.float32), my_slot, slot_count
-    ).astype(back.dtype)
-
-    for_partners(lambda dest: back_copy(dest).start())
-
     def lowrank_part(source):
         factor = jnp.concatenate(
             [down_ref[job_at(source, s)] for s in range(slot_count)], axis=0
@@ -363,7 +363,7 @@
         product = jnp.dot(factor, cols[source], preferred_element_type=jnp.float32)
         return pick_slots(product, token_rows(source)[0], slot_count)
 
-    def add_grads(source, right, first, rows, tiles=2):
+    def add_grads(source, right, first, rows, tiles=4):
         unused, job = token_rows(source)
 
         @pl.loop(0, half // (2 * tiles))

time: 172 us -> 168 us (0.977)
  Pallas kernels: 165 us -> 161 us
    pallas_call x1, Pallas kernels: 165 us -> 161 us  [local(): pl.pallas_call(functools.partial(exchange_kernel, owner), out_shape=(jax....]
where the time goes in v5:
time: 168 us
  Pallas kernels  161 us (96%)
  local copies, waits for them, and re-layouts  6.01 us (4%)
    pallas_call x1, Pallas kernels, local(): pl.pallas_call(functools.partial(exchange_kernel, owner), out_shape=(jax....  161 us
    unnamed x3, local copies, waits for them, and re-layouts  6.01 us

profile of v5, /device:TPU:31, one launch (start us, length us, event | category | flops | bytes accessed | tf_op | source)
XLA Modules:
  0.0 167.9 jit_solution(12199401196118960919)
XLA Ops:
  0.6 1.4 copy.8.device_jobs_ref
  2.0 161.3 %exchange.1 = (bf16[256,256]{1,0:T(8,128)(2,1)}, bf16[32,33792]{1,0:T(8,128)(2,1)}) custom-call(s32[64]{0:T(128)} %seq_slot_ref.1, s32[16,4]{1,0:T(8,128)} %copy.8.device_jobs_ref, bf16[256,8192]{1,0:T(8,128)(2,1)} %tokens_ref.1, bf16[8192,256]{1,0:T(8,128)(2,1)} %weight_ref.1, bf16[256,256]{1,0:T(8,128)(2,1)} %upstream_ref.1, bf16[32,33792]{1,0:T(8,128)(2,1)} %panels_ref.1), custom_call_target="tpu_custom_call" | custom-call | tf_op jit(solution)/shard_map/exchange/pallas_call | solution.py:485
  163.3 1.6 copy.11
  164.8 3.1 %copy.12 = bf16[32,33792]{1,0:T(8,128)(2,1)} copy(bf16[32,33792]{1,0:T(8,128)(2,1)} %get-tuple-element.5) | data formatting | bytes 4325376
